TPU v7x, 128 devices: a whole 4x4x4 slice. The times are simulated.
128 devices in a mesh: section: 4 (over z_hi, core), rep: 32 (over x, z_lo, y).
Axes of the slice: x: 4, y: 4, z: 4 (z_hi: 2, z_lo: 2; z = z_hi * 2 + z_lo), core: 2. Of those that a mesh axis runs over, the one named last changes fastest.
Arguments:
- micro_inputs: bfloat16 [2, 4096, 6144], P(None, 'rep'), may hold values from -6 to 6
- output_grads: bfloat16 [2, 4096, 6144], P(None, 'rep'), may hold values from -0.09375 to 0.09375
- stash: bfloat16 [4, 2, 2, 4096, 6144], P('section', None, None, 'rep'), may hold values from -6 to 6, as said below
- sample_ids: int32 [2, 32], P(None, 'rep'), may hold values from 0 to 1
- fwd_exps: int32 [4, 2, 4096, 48], P(None, None, 'rep'), may hold values from -1 to 2
- bwd_exps: int32 [4, 2, 4096, 48], P(None, None, 'rep'), may hold values from -13 to -10
- adapter_in: bfloat16 [4, 1, 6144, 128], P('section'), may hold values from -0.078125 to 0.078125
- adapter_out: bfloat16 [4, 1, 128, 6144], P('section'), may hold values from -0.5 to 0.5
Outputs:
- grad_in: bfloat16 [4, 1, 6144, 128], P('section')
- grad_out: bfloat16 [4, 1, 128, 6144], P('section')
Inputs may be any that keep to these rules, and one draw needn't show every extreme that they name: stash[s, 1] equals stash[s + 1, 0]: the stored output of a section is the stored input of the next.
All inputs are finite; a program needn't handle non-finite values.
Results may differ from a plain program's by a relative error of at most 0.014.
Values may be sent and summed in bfloat16 or wider, within the bound.
No kernel may reach another device: no remote copies, remote signals or barrier semaphores. Data moves between devices by JAX's collectives and lax.ppermute only.
A program may use at most 128 MiB of HBM per device.

v0:
```python
import functools

import jax
import jax.numpy as jnp
from jax import lax
from jax.experimental import pallas as pl
from jax.experimental.pallas import tpu as pltpu
from jax.sharding import PartitionSpec as P

EPS = 1e-05
BF = jnp.bfloat16
F32 = jnp.float32
ROWS = 16
LANES = 128
MIB = 1024 * 1024
ANY = pl.BlockSpec(memory_space=pl.ANY)
HBM = pl.BlockSpec(memory_space=pltpu.HBM)
VMEM = pl.BlockSpec(memory_space=pltpu.VMEM)
SMEM = pl.BlockSpec(memory_space=pltpu.SMEM)


def dot_nn(a, b):
    return lax.dot_general(a, b, (((1,), (0,)), ((), ())), preferred_element_type=F32)


def dot_nt(a, b):
    return lax.dot_general(a, b, (((1,), (1,)), ((), ())), preferred_element_type=F32)


def dot_tn(a, b):
    return lax.dot_general(a, b, (((0,), (0,)), ((), ())), preferred_element_type=F32)


class Place:
    def __init__(self, ids):
        rep = lax.axis_index("rep")
        self.ids = ids
        self.at = {0: lax.axis_index("section"), 3: rep // 8, 4: rep // 4 % 2, 5: rep % 4}

    def __getitem__(self, k):
        return self.ids[k - 1, 0] if k in (1, 2) else self.at[k]


def placed(body, ids, *refs):
    body(Place(ids), *refs)


def call(body, outs, scratch, ins, flops=10**8, nbytes=4 * 10**6, vmem=12, aliases=None):
    return pl.pallas_call(
        functools.partial(placed, body) if ins[0][1] is SMEM else body,
        out_shape=[jax.ShapeDtypeStruct(s, d) for s, d, _ in outs],
        in_specs=[spec for _, spec in ins],
        out_specs=[spec for _, _, spec in outs],
        scratch_shapes=scratch,
        input_output_aliases=aliases or {},
        compiler_params=pltpu.CompilerParams(vmem_limit_bytes=vmem * MIB),
        cost_estimate=pl.CostEstimate(flops=flops, bytes_accessed=nbytes, transcendentals=0),
    )(*[pltpu.with_memory_space_constraint(a, pltpu.HBM) if spec is HBM else a for a, spec in ins])


def lane_iota(rows):
    return lax.broadcasted_iota(jnp.int32, (rows, LANES), 1)


def row_iota(rows):
    return lax.broadcasted_iota(jnp.int32, (rows, LANES), 0)


def three(x):
    hi = x.astype(BF).astype(F32)
    rest = x - hi
    mid = rest.astype(BF).astype(F32)
    return hi, mid, (rest - mid).astype(BF).astype(F32)


def pack_rows(first_half, second_half, extra):
    at = row_iota(16)
    out = jnp.zeros((16, LANES), F32)
    for base, (a, b) in ((0, first_half), (8, second_half)):
        for j, row in enumerate(three(a) + three(b)):
            out = jnp.where(at == base + j, row, out)
    if extra is not None:
        hi, mid, _ = three(extra)
        out = jnp.where(at == 6, hi, out)
        out = jnp.where(at == 7, mid, out)
    return out.astype(BF)


def unpack_rows(block):
    block = block.astype(F32)

    def joined(base):
        return block[base : base + 1] + block[base + 1 : base + 2] + block[base + 2 : base + 3]

    return (joined(0), joined(8)), (joined(3), joined(11)), block[6:7] + block[7:8]


def columns(rows):
    at = row_iota(LANES)
    out = jnp.zeros((LANES, LANES), F32)
    for j, row in enumerate(rows):
        out = jnp.where(at == j, row, out)
    return out.T


def join_latent(msgs, tokens, width):
    parsed = [unpack_rows(m[tokens : tokens + 16]) for m in msgs]
    total = msgs[0][:tokens].astype(F32)
    for m in msgs[1:]:
        total = total + m[:tokens].astype(F32)
    halves = []
    for half in range(2):
        means = [p[0][half] for p in parsed]
        mean = (means[0] + means[1] + means[2] + means[3]) * 0.25
        offs = [m - mean for m in means]
        var = (parsed[0][1][half] + parsed[1][1][half] + parsed[2][1][half] + parsed[3][1][half]) * 0.25
        var = var + (offs[0] * offs[0] + offs[1] * offs[1] + offs[2] * offs[2] + offs[3] * offs[3]) * 0.25
        halves.append(columns([mean, lax.rsqrt(var + EPS)] + offs))
    cols = jnp.concatenate(halves, axis=0)
    colsum = parsed[0][2]
    for d in range(4):
        total = total + cols[:, 2 + d : 3 + d] * parsed[d][2]
        if d:
            colsum = colsum + parsed[d][2]
    return total * cols[:, 1:2], cols[:, 0:1], cols[:, 1:2], colsum


def start_first(pairs, sem):
    for cond, src, dst in pairs:
        @pl.when(cond)
        def _(src=src, dst=dst):
            pltpu.make_async_copy(src, dst, sem).start()


def start_weight(section, sc, own, near, same, cross, inner, dst, sem):
    q, x, y = sc[0], sc[3], sc[5]
    zh, c = q // 2, q % 2
    here = zh == section // 2
    mine = c == section % 2
    piece = 384

    def start(src, to):
        pltpu.make_async_copy(src, to, sem).start()

    @pl.when(here & mine)
    def _():
        start(own, dst)

    @pl.when(here & jnp.logical_not(mine))
    def _():
        start(near, dst)

    def pieces(refs, first):
        for j in range(2):
            for i in range(2):
                px, py = (i, j) if first == 0 else (j, i)
                at = piece_of(x ^ px, y ^ py) * piece
                base = i * 2 * piece
                if inner:
                    start(refs[j].at[pl.ds(base, piece)], dst.at[pl.ds(pl.multiple_of(at, piece), piece)])
                else:
                    for t in range(piece // LANES):
                        cols = pl.ds(pl.multiple_of(at + t * LANES, LANES), LANES)
                        start(refs[j].at[pl.ds(base + piece + t * LANES, LANES)], dst.at[:, cols])

    @pl.when(jnp.logical_not(here) & mine)
    def _():
        pieces(same, 0)

    @pl.when(jnp.logical_not(here) & jnp.logical_not(mine))
    def _():
        pieces(cross, 1)


def piece_of(x, y):
    return (x & 1) * 2 + (y & 1)


def factors(exps, q, out):
    every = exps.shape[0] // 2
    blocks = every // 4
    for k in range(4):
        @pl.when(q == k)
        def _(k=k):
            for m in range(2):
                e = exps[m * every + k * blocks : m * every + (k + 1) * blocks, :]
                f = lax.shift_left(jnp.ones(e.shape, jnp.int32), e + 14).astype(F32) * (2.0**-14)
                full = jnp.concatenate([f, jnp.zeros((LANES - blocks, LANES), F32)], axis=0)
                out[m * LANES : (m + 1) * LANES, :] = full.T


def wait_for(dst, sem):
    pltpu.make_async_copy(dst, dst, sem).wait()


def send_body(sc, stash, w_in, w_out, far, mid, sib_in, sib_out, over, sems):
    q, x, y = sc[0], sc[3], sc[5]
    c = q % 2
    tok, quarter = far.shape[0] // 2, far.shape[1]
    piece = quarter // 4
    mid_slot = jnp.where(q == 1, 1, 0)
    copies = []

    def go(src, dst):
        copy = pltpu.make_async_copy(src, dst, sems.at[len(copies)])
        copy.start()
        copies.append(copy)

    def cols(k):
        return pl.ds(pl.multiple_of((q ^ k) * quarter, quarter), quarter)

    for k in (2, 3):
        base = (q ^ k) * quarter + piece_of(x, y) * piece
        first = (k - 2) * 2 * piece
        go(w_in.at[0, 0, pl.ds(pl.multiple_of(base, piece), piece), :], over.at[pl.ds(first, piece)])
        for t in range(piece // LANES):
            from_cols = pl.ds(pl.multiple_of(base + t * LANES, LANES), LANES)
            go(w_out.at[0, 0, :, from_cols], over.at[pl.ds(first + piece + t * LANES, LANES)])
    for m in range(2):
        go(stash.at[0, 1 - c, sc[1 + m], :, cols(2)], far.at[pl.ds(m * tok, tok)])
    go(w_out.at[0, 0, :, cols(1)], sib_out)
    go(w_in.at[0, 0, cols(1), :], sib_in)
    for m in range(2):
        go(stash.at[0, mid_slot, sc[1 + m], :, cols(1)], mid.at[pl.ds(m * tok, tok)])
    for copy in copies:
        copy.wait()


def sum_blocks(block, count):
    parts = []
    for b in range(count):
        v = block(b)
        if b < 4:
            parts.append(v)
        else:
            parts[b % 4] = parts[b % 4] + v
    return (parts[0] + parts[1]) + (parts[2] + parts[3])


def first_body(sc, micro, grads, w_in, w_out, msg, x_v, w_v, wo_v, n_v, st, sems):
    q = sc[0]
    tokens, width = x_v.shape
    tok = tokens // 2
    blocks = width // LANES

    def load(src, wsrc, wdst):
        copies = [pltpu.make_async_copy(src.at[m], x_v.at[pl.ds(m * tok, tok)], sems.at[m]) for m in range(2)]
        copies.append(pltpu.make_async_copy(wsrc.at[0, 0], wdst, sems.at[2]))
        for copy in copies:
            copy.start()
        return copies

    @pl.when(q == 0)
    def _():
        load(micro, w_in, w_v)

    @pl.when(q == 3)
    def _():
        load(grads, w_out, wo_v)

    @pl.when((q == 1) | (q == 2))
    def _():
        msg[...] = jnp.zeros(msg.shape, BF)

    @pl.when(q == 0)
    def _():
        for m in range(2):
            wait_for(x_v.at[pl.ds(m * tok, tok)], sems.at[m])

            @pl.loop(m * (tok // ROWS), (m + 1) * (tok // ROWS), unroll=2)
            def _(i):
                rows = pl.ds(pl.multiple_of(i * ROWS, ROWS), ROWS)

                def block(b):
                    return x_v[rows, b * LANES : (b + 1) * LANES].astype(F32)

                def square(b):
                    d = block(b) - mean
                    return d * d

                mean = jnp.sum(sum_blocks(block, blocks), axis=1, keepdims=True) * (1.0 / width)
                mean = jnp.broadcast_to(mean, (ROWS, LANES))
                inv = lax.rsqrt(jnp.sum(sum_blocks(square, blocks), axis=1, keepdims=True) * (1.0 / width) + EPS)
                inv = jnp.broadcast_to(inv, (ROWS, LANES))
                for b in range(blocks):
                    n_v[rows, b * LANES : (b + 1) * LANES] = ((block(b) - mean) * inv).astype(BF)
                st[rows, :] = jnp.where(lane_iota(ROWS) == 0, mean, inv)

        wait_for(w_v, sems.at[2])
        latent = dot_nn(n_v[...], w_v[...])
        msg[:tokens] = latent.astype(BF)
        t0, t1 = st[:LANES].T, st[LANES:].T
        msg[tokens:] = pack_rows((t0[0:1], t0[1:2]), (t1[0:1], t1[1:2]), None)

    @pl.when(q == 3)
    def _():
        for m in range(2):
            wait_for(x_v.at[pl.ds(m * tok, tok)], sems.at[m])
        wait_for(wo_v, sems.at[2])
        msg[:tokens] = dot_nt(x_v[...], wo_v[...]).astype(BF)
        msg[tokens:] = jnp.zeros((msg.shape[0] - tokens, msg.shape[1]), BF)


def forward_body(section, sc, *refs):
    first = section == 1
    refs = list(refs)
    take = refs.pop
    msgs = [take(0) for _ in range(4)]
    h_in = take(0)
    exps = take(0)
    stash, held = take(0), take(0)
    wi_own, wo_own, wi_near, wo_near = [take(0) for _ in range(4)]
    same, cross = [take(0) for _ in range(2)], [take(0) for _ in range(2)]
    h_out, normed, msg, latf, invb, colsum_out, wo_v, wi_v = [take(0) for _ in range(8)]
    x_v, pick, up, cen, st, mc = [take(0) for _ in range(6)]
    lat_v, e_v, factor, sems = [take(0) for _ in range(4)]
    q = sc[0]
    c = q % 2
    tokens, quarter = pick.shape
    tok = tokens // 2
    cols = pl.ds(pl.multiple_of(q * quarter, quarter), quarter)
    start_weight(section - 1, sc, wo_own.at[0, 0, :, cols], wo_near, same, cross, False, wo_v, sems.at[0])
    for m in range(2):
        pltpu.make_async_copy(exps.at[section - 1, m], e_v.at[pl.ds(m * exps.shape[2], exps.shape[2])], sems.at[4]).start()
    if first:
        for m in range(2):
            pltpu.make_async_copy(h_in.at[m, :, cols], x_v.at[pl.ds(m * tok, tok)], sems.at[2]).start()
    if section == 2:
        local, slot = (q == 1) | (q == 2), jnp.where(q == 1, 1, 0)
    else:
        local, slot = (q // 2 == 0) if section == 1 else (q // 2 == 1), 1 - c
    for m in range(2):
        rows = pl.ds(m * tok, tok)
        start_first(
            [
                (local, stash.at[0, slot, sc[1 + m], :, cols], pick.at[rows]),
                (jnp.logical_not(local), held.at[rows], pick.at[rows]),
            ],
            sems.at[3],
        )
    start_weight(section, sc, wi_own.at[0, 0, cols, :], wi_near, same, cross, True, wi_v, sems.at[1])

    if first:
        for k in range(4):
            @pl.when(q == k)
            def _(k=k):
                lat_v[...] = msgs[k][...]

        (m0, m1), (v0, v1), _ = unpack_rows(lat_v[tokens:])
        both = jnp.concatenate([columns([m0, v0]), columns([m1, v1])], axis=0)
        latent = lat_v[:tokens].astype(F32)
        mean, inv = both[:, 0:1], both[:, 1:2]
        colsum_out[...] = jnp.zeros(colsum_out.shape, F32)
    else:
        latent, mean, inv, colsum = join_latent([m[...] for m in msgs], tokens, quarter)
        colsum_out[...] = jnp.broadcast_to(colsum, colsum_out.shape)
    latf[...] = latent
    invb[...] = jnp.broadcast_to(inv, invb.shape)
    mc[...] = jnp.broadcast_to(mean, mc.shape)
    wait_for(wo_v, sems.at[0])
    up[...] = dot_nn(latent.astype(BF), wo_v[...])
    wait_for(e_v, sems.at[4])
    factors(e_v, q, factor)
    if first:
        wait_for(x_v, sems.at[2])
        src = x_v
    else:
        src = h_in
    wait_for(pick, sems.at[3])

    @pl.loop(0, tokens // ROWS, unroll=4)
    def _(i):
        rows = pl.ds(pl.multiple_of(i * ROWS, ROWS), ROWS)
        mean_t, inv_t = mc[rows, :], invb[rows, :]
        fac = factor[rows, :]
        kept = []
        for b in range(quarter // LANES):
            lanes = slice(b * LANES, (b + 1) * LANES)
            h = src[rows, lanes].astype(F32)
            normed[rows, lanes] = ((h - mean_t) * inv_t).astype(BF)
            stored = pick[rows, lanes].astype(F32)
            f = fac[:, b : b + 1]
            d = jnp.clip(h + up[rows, lanes] - stored, f * -8.0, f * 7.0).astype(BF)
            h = stored + d.astype(F32)
            h_out[rows, lanes] = h
            kept.append(h)
        st[rows, :] = sum_blocks(lambda b: kept[b], quarter // LANES)

    mean_d = jnp.sum(st[...], axis=1, keepdims=True) * (1.0 / quarter)
    mc[...] = jnp.broadcast_to(mean_d, mc.shape)

    @pl.loop(0, tokens // ROWS, unroll=4)
    def _(i):
        rows = pl.ds(pl.multiple_of(i * ROWS, ROWS), ROWS)
        mean_t = mc[rows, :]
        kept = [h_out[rows, b * LANES : (b + 1) * LANES] - mean_t for b in range(quarter // LANES)]
        for b in range(quarter // LANES):
            cen[rows, b * LANES : (b + 1) * LANES] = kept[b].astype(BF)
        st[rows, :] = sum_blocks(lambda b: kept[b] * kept[b], quarter // LANES)

    var_d = jnp.sum(st[...], axis=1, keepdims=True) * (1.0 / quarter)
    st[...] = jnp.where(lane_iota(tokens) == 0, mc[...], var_d)

    wait_for(wi_v, sems.at[1])
    w = wi_v[...]
    msg[:tokens] = dot_nn(cen[...], w).astype(BF)
    colsum = dot_nn(jnp.ones((16, quarter), BF), w)[0:1]
    t0, t1 = st[:LANES].T, st[LANES:].T
    msg[tokens:] = pack_rows((t0[0:1], t0[1:2]), (t1[0:1], t1[1:2]), colsum)


def backward_body(section, sc, *refs):
    top = section == 3
    refs = list(refs)
    take = refs.pop
    msgs = [take(0) for _ in range(4)]
    if top:
        lat_msgs = [take(0) for _ in range(4)]
        h_in = take(0)
    else:
        normed_in, latf, invb, colsum_in = [take(0) for _ in range(4)]
    g_in = take(0)
    exps, wo_v, wi_v = [take(0) for _ in range(3)]
    g_out, msg, glat_out = [take(0) for _ in range(3)]
    if top:
        normed, latf, g_v = [take(0) for _ in range(3)]
    gn, mc, inv_v, a_v, b_v, e_v, factor, sems = [take(0) for _ in range(8)]
    q = sc[0]
    tokens, quarter = gn.shape
    tok = tokens // 2
    width = 4 * quarter
    cols = pl.ds(pl.multiple_of(q * quarter, quarter), quarter)
    for m in range(2):
        pltpu.make_async_copy(exps.at[section, m], e_v.at[pl.ds(m * exps.shape[2], exps.shape[2])], sems.at[1]).start()
    if top:
        for m in range(2):
            pltpu.make_async_copy(g_in.at[m, :, cols], g_v.at[pl.ds(m * tok, tok)], sems.at[0]).start()
        latent, mean, inv, colsum = join_latent([m[...] for m in lat_msgs], tokens, quarter)
        latf[...] = latent
        mc[...] = jnp.broadcast_to(mean, mc.shape)
        inv_v[...] = jnp.broadcast_to(inv, inv_v.shape)
        for k in range(4):
            @pl.when(q ^ 3 == k)
            def _(k=k):
                glat_out[...] = msgs[k][:tokens]

        glat = glat_out[...]
        src, norm, inv_ref = g_v, normed, inv_v
    else:
        latent, colsum = latf[...], colsum_in[0:1]
        glat = msgs[0][:tokens].astype(F32)
        for m in msgs[1:]:
            glat = glat + m[:tokens].astype(F32)
        glat = glat.astype(BF)
        glat_out[...] = glat
        src, norm, inv_ref = g_in, normed_in, invb
    wide = glat.astype(F32)
    a_v[...] = jnp.broadcast_to(jnp.sum(wide * colsum, axis=1, keepdims=True) * (1.0 / width), a_v.shape)
    b_v[...] = jnp.broadcast_to(jnp.sum(wide * latent, axis=1, keepdims=True) * (1.0 / width), b_v.shape)
    gn[...] = dot_nt(glat, wi_v[...])
    wait_for(e_v, sems.at[1])
    factors(e_v, q, factor)
    if top:
        wait_for(g_v, sems.at[0])

    @pl.loop(0, tokens // ROWS, unroll=4)
    def _(i):
        rows = pl.ds(pl.multiple_of(i * ROWS, ROWS), ROWS)
        fac = factor[rows, :]
        inv_t, a_t, b_t = inv_ref[rows, :], a_v[rows, :], b_v[rows, :]
        for b in range(quarter // LANES):
            lanes = slice(b * LANES, (b + 1) * LANES)
            if top:
                n = (h_in[rows, lanes] - mc[rows, :]) * inv_t
                normed[rows, lanes] = n.astype(BF)
            else:
                n = norm[rows, lanes].astype(F32)
            f = fac[:, b : b + 1]
            g = src[rows, lanes].astype(F32) + inv_t * (gn[rows, lanes] - a_t - n * b_t)
            g_out[rows, lanes] = jnp.clip(g, f * -128.0, f * 127.0).astype(BF)

    msg[...] = dot_nt(g_out[...], wo_v[...]).astype(BF)


def grads_body(normed, latf, g_ref, glat, gin, gout):
    gin[...] = dot_tn(normed[...], glat[...]).astype(BF)
    gout[...] = dot_tn(latf[...].astype(BF), g_ref[...]).astype(BF)


def grads_top_body(sc, normed, latf, g_ref, glat, gin, gout, g_v, sems):
    quarter = g_v.shape[1]
    tok = g_v.shape[0] // 2
    cols = pl.ds(pl.multiple_of(sc[0] * quarter, quarter), quarter)
    for m in range(2):
        pltpu.make_async_copy(g_ref.at[m, :, cols], g_v.at[pl.ds(m * tok, tok)], sems.at[0]).start()
    gin[...] = dot_tn(normed[...], glat[...]).astype(BF)
    wait_for(g_v, sems.at[0])
    gout[...] = dot_tn(latf[...].astype(BF), g_v[...]).astype(BF)


def grads_first_body(sc, *refs):
    refs = list(refs)
    take = refs.pop
    msgs = [take(0) for _ in range(4)]
    normed, latf, g_ref = [take(0) for _ in range(3)]
    gins = [None] + [take(0) for _ in range(3)]
    gouts = [None] + [take(0) for _ in range(3)]
    a, b = [take(0) for _ in range(5)], [take(0) for _ in range(5)]
    gin0, gout0 = take(0), take(0)
    gins[0], gouts[0] = gin0, gout0
    x, y = sc[3], sc[5]
    glat = msgs[0][...].astype(F32)
    for m in msgs[1:]:
        glat = glat + m[...].astype(F32)
    gin0[...] = dot_tn(normed[...], glat.astype(BF)).astype(BF)
    gout0[...] = dot_tn(latf[...].astype(BF), g_ref[...]).astype(BF)
    rows, low = a[0].shape[1], b[0].shape[1]
    for k in range(4):
        at = pl.ds(pl.multiple_of(((x + k) % 4) * rows, rows), rows)
        to = pl.ds(pl.multiple_of(((y + k) % 4) * low, low), low)
        for s in range(4):
            d, i = (2 + s // 2, s % 2) if k == 2 else ((0, 1, 2, 4)[k], s)
            a[d][i] = gins[s][at, :]
            b[d][i] = gouts[s][to, :]


def relay_body(a1, a3, a_lo, a_hi, b1, b3, b_lo, b_hi, a1_out, a3_out, b1_out, b3_out):
    for src, extra, at, dst in (
        (a1, a_lo, 0, a1_out),
        (a3, a_hi, 2, a3_out),
        (b1, b_lo, 0, b1_out),
        (b3, b_hi, 2, b3_out),
    ):
        for s in range(4):
            if at <= s < at + 2:
                dst[s] = total_of([src[s], extra[s - at]])
            else:
                dst[s] = src[s]


def total_of(parts):
    total = parts[0].astype(F32)
    for part in parts[1:]:
        total = total + part.astype(F32)
    return total.astype(BF)


def second_body(sc, a0, a1, a2, b0, b1, b2, c0, c1, c2, c3, d0, d1, d2, d3, a_v, b_v):
    x, y = sc[3], sc[5]
    for s in range(4):
        a_v[s] = total_of([r[s] for r in (a0, a1, a2)])
        b_v[s] = total_of([r[s] for r in (b0, b1, b2)])
    rows, cols = c0.shape[1], d0.shape[2]
    for k, (c, d) in enumerate(((c0, d0), (c1, d1), (c2, d2), (c3, d3))):
        at = pl.ds(pl.multiple_of(((y + k) % 4) * rows, rows), rows)
        to = pl.ds(pl.multiple_of(((x + k) % 4) * cols, cols), cols)
        for s in range(4):
            c[s] = a_v[s, at, :]
            d[s] = b_v[s, :, to]


def third_body(a0, a1, a2, a3, b0, b1, b2, b3, out):
    rows, low = a0.shape[1], b0.shape[1]
    for s in range(4):
        out[s, :rows] = total_of([r[s] for r in (a0, a1, a2, a3)])
        total = total_of([r[s] for r in (b0, b1, b2, b3)])
        for t in range(total.shape[1] // LANES):
            out[s, rows + t * low : rows + (t + 1) * low] = total[:, t * LANES : (t + 1) * LANES]


def rep_of(x, z, y):
    return x * 8 + z * 4 + y


EVERY = [(x, z, y) for x in range(4) for z in range(2) for y in range(4)]


def along_x(value, k):
    return lax.ppermute(value, "rep", [(rep_of(x, z, y), rep_of((x + k) % 4, z, y)) for x, z, y in EVERY])


def along_y(value, k):
    return lax.ppermute(value, "rep", [(rep_of(x, z, y), rep_of(x, z, (y + k) % 4)) for x, z, y in EVERY])


def along_z(value, k):
    return lax.ppermute(value, "rep", [(rep_of(x, z, y), rep_of(x, (z + k) % 2, y)) for x, z, y in EVERY])


def gather(value, count, move):
    return [value] + [move(value, k) for k in range(1, count)]


def gather_relayed(value, move):
    before, after = move(value, 1), move(value, 3)
    half = value.shape[0] // 2
    return [value, before, move(before[:half], 1), move(after[half:], 3), after]


def place_pieces(sc, parts, gin, gout, gin_v, gout_v, sem):
    q, x, y = sc[0], sc[3], sc[5]
    quarter = gin.shape[2] // 4
    rows, low = quarter // 16, gout.shape[2] // 4
    copies = []
    for back, first, a_ref, b_ref in parts:
        for i in range(a_ref.shape[0]):
            j = first + i
            for d in range(4):
                base = (q ^ d) * quarter
                row = base + ((x - back + 4) % 4) * (quarter // 4) + ((y - j + 4) % 4) * rows
                gin_v[pl.ds(pl.multiple_of(row, rows), rows), :] = a_ref[i, d]
                at = pl.ds(pl.multiple_of(((y - back + 4) % 4) * low, low), low)
                for t in range(quarter // 4 // LANES):
                    col = base + ((x - j + 4) % 4) * (quarter // 4) + t * LANES
                    gout_v[at, pl.ds(pl.multiple_of(col, LANES), LANES)] = b_ref[i, d, t * low : (t + 1) * low, :]
        if first + a_ref.shape[0] == 4:
            for d in range(4):
                row = d * quarter + ((x - back + 4) % 4) * (quarter // 4)
                whole = pl.ds(pl.multiple_of(row, quarter // 4), quarter // 4)
                copies.append(pltpu.make_async_copy(gin_v.at[whole], gin.at[0, 0, whole], sem.at[len(copies)]))
                copies[-1].start()
            whole = pl.ds(pl.multiple_of(((y - back + 4) % 4) * low, low), low)
            copies.append(pltpu.make_async_copy(gout_v.at[whole], gout.at[0, 0, whole], sem.at[len(copies)]))
            copies[-1].start()
    for copy in copies:
        copy.wait()


def place_body(sc, a0, a1, a4, b0, b1, b4, gin, gout, gin_v, gout_v, sem):
    place_pieces(sc, ((0, 0, a0, b0), (1, 0, a1, b1), (3, 0, a4, b4)), gin, gout, gin_v, gout_v, sem)


def place_last_body(sc, a2, a3, b2, b3, gin_in, gout_in, gin, gout, gin_v, gout_v, sem):
    place_pieces(sc, ((2, 0, a2, b2), (2, 2, a3, b3)), gin, gout, gin_v, gout_v, sem)


def on_device(micro, grads, stash, sample_ids, fwd_exps, bwd_exps, w_in, w_out):
    q = lax.axis_index("section")
    tok, width = micro.shape[1], micro.shape[2]
    tokens, quarter, rank = 2 * tok, width // 4, w_in.shape[3]
    fwd_exps, bwd_exps = jnp.swapaxes(fwd_exps, 2, 3), jnp.swapaxes(bwd_exps, 2, 3)
    sc = sample_ids

    def swap(value, k, sources=range(4)):
        return lax.ppermute(value, "section", [(s, s ^ k) for s in sources])

    def exchange(value):
        return [value] + [swap(value, k) for k in (1, 2, 3)]

    def beside(value):
        pairs = [(s * 32 + rep_of(xx, zz, yy), (s ^ 2) * 32 + rep_of(xx, 1 - zz, yy)) for s in range(4) for xx, zz, yy in EVERY]
        return lax.ppermute(value, ("section", "rep"), pairs)

    def beside_along(value, dx, dy, core):
        pairs = [(s * 32 + rep_of(xx, zz, yy), (s ^ core) * 32 + rep_of(xx ^ dx, zz, yy ^ dy)) for s in range(4) for xx, zz, yy in EVERY]
        return lax.ppermute(value, ("section", "rep"), pairs)

    dma = pltpu.SemaphoreType.DMA
    big = (tokens, quarter)
    qi, qo = (quarter, rank), (rank, quarter)
    far, mid, sib_in, sib_out, over = call(
        send_body,
        [(big, BF, VMEM)] * 2 + [(qi, BF, VMEM), (qo, BF, VMEM), (qi, BF, VMEM)],
        [dma((14,))],
        [(sc, SMEM), (stash, HBM), (w_in, HBM), (w_out, HBM)],
    )
    over = beside(over)
    (msg0,) = call(
        first_body,
        [((tokens + 16, rank), BF, VMEM)],
        [
            pltpu.VMEM((tokens, width), BF),
            pltpu.VMEM((width, rank), BF),
            pltpu.VMEM((rank, width), BF),
            pltpu.VMEM((tokens, width), BF),
            pltpu.VMEM((tokens, LANES), F32),
            dma((3,)),
        ],
        [(sc, SMEM), (micro, HBM), (grads, HBM), (w_in, HBM), (w_out, HBM)],
        vmem=16,
        nbytes=3 * 10**7,
    )
    msg0, far = lax.optimization_barrier((msg0, far))
    far = swap(far, 2)
    near_msg = swap(msg0, 1, (0, 3))
    over, msg0, sib_in, sib_out = lax.optimization_barrier((over, msg0, sib_in, sib_out))
    half = quarter // 2
    same, cross = over[:half], over[half:]
    same = jnp.concatenate([same, beside_along(same, 1, 0, 0)], 0)
    cross = jnp.concatenate([swap(cross, 1), beside_along(cross, 0, 1, 1)], 0)
    same, cross, sib_in, sib_out = lax.optimization_barrier((same, cross, sib_in, sib_out))
    pieces = [same, beside_along(same, 0, 1, 0), cross, beside_along(cross, 1, 0, 0)]
    near = [swap(sib_in, 1), swap(sib_out, 1)]
    near, msg0 = lax.optimization_barrier((near, msg0))
    msgs0 = [near_msg] + [swap(msg0, k, (0, 3)) for k in (2, 3)]
    pieces, far, near, msgs0 = lax.optimization_barrier((pieces, far, near, msgs0))
    msgs0 = [msg0] + msgs0
    weights = [w_in, w_out] + near + pieces
    weights = list(zip(weights, [HBM, HBM] + [ANY] * 6))

    msgs = msgs0
    h = micro
    kept = []
    held = {}
    for section in (1, 2, 3):
        h, normed, msg, latf, invb, colsum, low_out, high_in = call(
            functools.partial(forward_body, section),
            [
                (big, F32, VMEM),
                (big, BF, VMEM),
                ((tokens + 16, rank), BF, VMEM),
                ((tokens, rank), F32, VMEM),
                ((tokens, LANES), F32, VMEM),
                ((8, LANES), F32, VMEM),
                (qo, BF, VMEM),
                (qi, BF, VMEM),
            ],
            [
                pltpu.VMEM(big, BF),
                pltpu.VMEM(big, BF),
                pltpu.VMEM(big, F32),
                pltpu.VMEM(big, BF),
                pltpu.VMEM((tokens, LANES), F32),
                pltpu.VMEM((tokens, LANES), F32),
                pltpu.VMEM((tokens + 16, rank), BF),
                pltpu.VMEM((2 * fwd_exps.shape[2], tok), jnp.int32),
                pltpu.VMEM((tokens, LANES), F32),
                dma((5,)),
            ],
            [(sc, SMEM)]
            + [(m, VMEM) for m in msgs]
            + [(h, HBM if section == 1 else VMEM), (fwd_exps, HBM), (stash, HBM)]
            + [(mid if section == 2 else far, ANY)]
            + weights,
        )
        kept.append((normed, latf, invb, colsum))
        held[section] = [low_out, high_in]
        if section == 1:
            msg, mid = lax.optimization_barrier((msg, mid))
            mid = swap(mid, 1, (1, 2))
        msgs = exchange(msg)

    gins, gouts = {}, {}
    g = grads
    for section in (3, 2, 1):
        top = section == 3
        outs = [(big, BF, VMEM), ((tokens, rank), BF, VMEM), ((tokens, rank), BF, VMEM)]
        scratch = [
            pltpu.VMEM(big, F32),
            pltpu.VMEM((tokens, LANES), F32),
            pltpu.VMEM((tokens, LANES), F32),
            pltpu.VMEM((tokens, LANES), F32),
            pltpu.VMEM((tokens, LANES), F32),
            pltpu.VMEM((2 * bwd_exps.shape[2], tok), jnp.int32),
            pltpu.VMEM((tokens, LANES), F32),
            dma((2,)),
        ]
        if top:
            outs += [(big, BF, VMEM), ((tokens, rank), F32, VMEM)]
            scratch = [pltpu.VMEM(big, BF)] + scratch
            ins = [(m, VMEM) for m in msgs0] + [(m, VMEM) for m in msgs] + [(h, VMEM), (g, HBM)]
        else:
            ins = [(m, VMEM) for m in msgs] + [(v, VMEM) for v in kept[section]] + [(g, VMEM)]
        result = call(
            functools.partial(backward_body, section),
            outs,
            scratch,
            [(sc, SMEM)] + ins + [(bwd_exps, HBM)] + [(w, VMEM) for w in held[section]],
        )
        next_g, msg, glat = result[:3]
        if top:
            normed, latf = result[3:]
            gin, gout = call(
                grads_top_body,
                [(qi, BF, VMEM), (qo, BF, VMEM)],
                [pltpu.VMEM(big, BF), dma((1,))],
                [(sc, SMEM), (normed, VMEM), (latf, VMEM), (g, HBM), (glat, VMEM)],
            )
        else:
            normed, latf = kept[section][:2]
            gin, gout = call(
                grads_body,
                [(qi, BF, VMEM), (qo, BF, VMEM)],
                [],
                [(normed, VMEM), (latf, VMEM), (g, VMEM), (glat, VMEM)],
            )
        msgs = exchange(msg)
        gins[section], gouts[section] = gin, gout
        if section == 2:
            msgs, gins, gouts = lax.optimization_barrier((msgs, gins, gouts))
        g = next_g
    rows, low = quarter // 4, rank // 4
    cut = call(
        grads_first_body,
        [((n, rows, rank), BF, VMEM) for n in (4, 4, 2, 2, 4)] + [((n, low, quarter), BF, VMEM) for n in (4, 4, 2, 2, 4)],
        [pltpu.VMEM(qi, BF), pltpu.VMEM(qo, BF)],
        [(sc, SMEM)]
        + [(m, VMEM) for m in msgs]
        + [(kept[0][0], VMEM), (kept[0][1], VMEM), (g, VMEM)]
        + [(terms[s], VMEM) for terms in (gins, gouts) for s in (1, 2, 3)],
    )
    a, b = cut[:5], cut[5:]
    far_a, far_b = (along_x(a[2], 1), along_x(a[3], 3)), (along_y(b[2], 1), along_y(b[3], 3))
    to_a, back_a, to_b, back_b = call(
        relay_body,
        [((4, rows, rank), BF, VMEM)] * 2 + [((4, low, quarter), BF, VMEM)] * 2,
        [],
        [(v, VMEM) for v in (a[1], a[4], *far_a, b[1], b[4], *far_b)],
    )
    a = [a[0], along_x(to_a, 1), along_x(back_a, 3)]
    b = [b[0], along_y(to_b, 1), along_y(back_b, 3)]
    cut = call(
        second_body,
        [((4, rows // 4, rank), BF, VMEM)] * 4 + [((4, low, rows), BF, VMEM)] * 4,
        [pltpu.VMEM((4, rows, rank), BF), pltpu.VMEM((4, low, quarter), BF)],
        [(sc, SMEM)] + [(v, VMEM) for v in a + b],
    )
    a = [cut[0]] + [along_y(cut[k], k) for k in (1, 2, 3)]
    b = [cut[4]] + [along_x(cut[4 + k], k) for k in (1, 2, 3)]
    (both,) = call(
        third_body,
        [((4, rows // 2, rank), BF, VMEM)],
        [],
        [(v, VMEM) for v in a + b],
    )
    shares = (both.astype(F32) + along_z(both, 1).astype(F32)).astype(BF)
    own = [lax.dynamic_index_in_dim(shares, q ^ k, 0, keepdims=False) for k in range(4)]
    mine = jnp.stack([own[0]] + [swap(own[k], k) for k in (1, 2, 3)])
    a, b = mine[:, : rows // 4], mine[:, rows // 4 :]
    a, b = gather(a, 4, along_y), gather(b, 4, along_x)
    a, b = jnp.stack(a), jnp.stack(b)
    a, b = gather_relayed(a, along_x), gather_relayed(b, along_y)
    totals = [((1, 1, width, rank), BF, HBM), ((1, 1, rank, width), BF, HBM)]
    whole = [pltpu.VMEM((width, rank), BF), pltpu.VMEM((rank, width), BF)]
    total_in, total_out = call(
        place_body,
        totals,
        whole + [dma((15,))],
        [(sc, SMEM)] + [(v, VMEM) for v in (a[0], a[1], a[4], b[0], b[1], b[4])],
    )
    total_in, total_out = call(
        place_last_body,
        totals,
        whole + [dma((5,))],
        [(sc, SMEM)] + [(v, VMEM) for v in (a[2], a[3], b[2], b[3])] + [(total_in, HBM), (total_out, HBM)],
        aliases={5: 0, 6: 1},
    )
    return total_in, total_out


def solution(mesh):
    placed = (
        P(None, "rep", None),
        P(None, "rep", None),
        P("section", None, None, "rep", None),
        P(None, "rep"),
        P(None, None, "rep", None),
        P(None, None, "rep", None),
        P("section", None, None, None),
        P("section", None, None, None),
    )
    return jax.shard_map(
        on_device,
        mesh=mesh,
        in_specs=placed,
        out_specs=(P("section", None, None, None), P("section", None, None, None)),
        check_vma=False,
    )
```

profile of v0, /device:TPU:64, one launch (start us, length us, event | category | flops | bytes accessed | tf_op | source)
XLA Modules:
  0.0 199.8 jit_solution(11635576112060227662)
XLA Ops:
  1.4 2.5 %shard_map.95 = (bf16[256,1536]{1,0:T(8,128)(2,1)S(1)}, bf16[256,1536]{1,0:T(8,128)(2,1)S(1)}, bf16[1536,128]{1,0:T(8,128)(2,1)S(1)}, bf16[128,1536]{1,0:T(8,128)(2,1)S(1)}, bf16[1536,128]{1,0:T(8,128)(2,1)S(1)}) custom-call(s32[2,1]{1,0:T(2,128)S(1)} %copy.24.ids, bf16[1,2,2,128,6144]{4,3,2,1,0:T(8,128)(2,1)} %refs_6_.5, bf16[1,1,6144,128]{3,2,1,0:T(8,128)(2,1)} %refs_8_.5, ...), custom_call_target="tpu_custom_call" | custom-call | flops 100000000 | bytes 4000000 | tf_op jit(solution)/shard_map/pallas_call | solution.py:49
  4.7 10.1 %collective-permute-done = bf16[1536,128]{1,0:T(8,128)(2,1)S(1)} collective-permute-done((bf16[1536,128]{1,0:T(8,128)(2,1)S(1)}, bf16[1536,128]{1,0:T(8,128)(2,1)S(1)}, u32[]{:S(2)}, u32[]{:S(2)}) %collective-permute-start) | collective-permute-done | bytes 393248 | tf_op jit(solution)/shard_map/ppermute | solution.py:652
  16.4 1.9 collective-permute-start.8
  18.4 1.7 collective-permute-start.3
  20.7 4.2 %collective-permute-done.3 = bf16[768,128]{1,0:T(8,128)(2,1)S(1)} collective-permute-done((bf16[768,128]{1,0:T(8,128)(2,1)S(1)}, bf16[768,128]{1,0:T(8,128)(2,1)S(1)}, u32[]{:S(2)}, u32[]{:S(2)}) %collective-permute-start.3) | collective-permute-done | bytes 196640 | tf_op jit(solution)/shard_map/ppermute | solution.py:656
  31.8 4.2 %collective-permute-done.8.refs_7_ = bf16[256,1536]{1,0:T(8,128)(2,1)S(1)} collective-permute-done((bf16[256,1536]{1,0:T(8,128)(2,1)S(1)}, bf16[256,1536]{1,0:T(8,128)(2,1)S(1)}, u32[]{:S(2)}, u32[]{:S(2)}) %collective-permute-start.8) | collective-permute-done | bytes 786464 | tf_op jit(solution)/shard_map/ppermute | solution.py:645
  38.6 4.7 %shard_map.97 = (f32[256,1536]{1,0:T(8,128)S(1)}, bf16[256,1536]{1,0:T(8,128)(2,1)S(1)}, bf16[272,128]{1,0:T(8,128)(2,1)S(1)}, f32[256,128]{1,0:T(8,128)S(1)}, f...) custom-call(s32[2,1]{1,0:T(2,128)S(1)} %copy.24.ids, ...), custom_call_target="tpu_custom_call" | custom-call | flops 100000000 | bytes 4000000 | tf_op jit(solution)/shard_map/pallas_call | solution.py:49
  43.3 2.8 %collective-permute-start.15 = (bf16[256,1536]{1,0:T(8,128)(2,1)S(1)}, bf16[256,1536]{1,0:T(8,128)(2,1)S(1)}, u32[]{:S(2)}, u32[]{:S(2)}) collective-permute-start(bf16[256,1536]{1,0:T(8,128)(2,1)S(1)} %get-tuple-element.134), channel_id=1, source_target_pairs={{32,0},{64,96},{33,1},{65,97},{34,2},{66,98},{35,3},{67,99},{36,4}... | collective-permute-start | bytes 2359304 | tf_op jit(solution)/shard_map/ppermute | solution.py:645
  46.3 2.5 %collective-permute-start.13 = (bf16[272,128]{1,0:T(8,128)(2,1)S(1)}, bf16[272,128]{1,0:T(8,128)(2,1)S(1)}, u32[]{:S(2)}, u32[]{:S(2)}) collective-permute-start(bf16[272,128]{1,0:T(8,128)(2,1)S(1)} %get-tuple-element.132.refs_0_), channel_id=1, source_target_pairs={{0,64},{32,96},{64,0},{96,32},{1,65},{33,97},{65,1},{97,33},{2,66}... | collective-permute-start | bytes 208904 | tf_op jit(solution)/shard_map/ppermute | solution.py:645
  49.6 2.7 %collective-permute-done.13.refs_2_ = bf16[272,128]{1,0:T(8,128)(2,1)S(1)} collective-permute-done((bf16[272,128]{1,0:T(8,128)(2,1)S(1)}, bf16[272,128]{1,0:T(8,128)(2,1)S(1)}, u32[]{:S(2)}, u32[]{:S(2)}) %collective-permute-start.13) | collective-permute-done | bytes 69664 | tf_op jit(solution)/shard_map/ppermute | solution.py:645
  52.4 2.4 %collective-permute-done.14.refs_3_ = bf16[272,128]{1,0:T(8,128)(2,1)S(1)} collective-permute-done((bf16[272,128]{1,0:T(8,128)(2,1)S(1)}, bf16[272,128]{1,0:T(8,128)(2,1)S(1)}, u32[]{:S(2)}, u32[]{:S(2)}) %collective-permute-start.14) | collective-permute-done | bytes 69664 | tf_op jit(solution)/shard_map/ppermute | solution.py:645
  54.7 3.8 %shard_map.98 = (f32[256,1536]{1,0:T(8,128)S(1)}, bf16[256,1536]{1,0:T(8,128)(2,1)S(1)}, bf16[272,128]{1,0:T(8,128)(2,1)S(1)}, f32[256,128]{1,0:T(8,128)S(1)}, f...) custom-call(s32[2,1]{1,0:T(2,128)S(1)} %copy.24.ids, ...), custom_call_target="tpu_custom_call" | custom-call | flops 100000000 | bytes 4000000 | tf_op jit(solution)/shard_map/pallas_call | solution.py:49
  62.1 2.9 %collective-permute-done.17.refs_2_ = bf16[272,128]{1,0:T(8,128)(2,1)S(1)} collective-permute-done((bf16[272,128]{1,0:T(8,128)(2,1)S(1)}, bf16[272,128]{1,0:T(8,128)(2,1)S(1)}, u32[]{:S(2)}, u32[]{:S(2)}) %collective-permute-start.17) | collective-permute-done | bytes 69664 | tf_op jit(solution)/shard_map/ppermute | solution.py:645
  66.3 4.2 %shard_map.99 = (f32[256,1536]{1,0:T(8,128)S(1)}, bf16[256,1536]{1,0:T(8,128)(2,1)S(1)}, bf16[272,128]{1,0:T(8,128)(2,1)S(1)}, f32[256,128]{1,0:T(8,128)S(1)}, f...) custom-call(s32[2,1]{1,0:T(2,128)S(1)} %copy.24.ids, ...), custom_call_target="tpu_custom_call" | custom-call | flops 100000000 | bytes 4000000 | tf_op jit(solution)/shard_map/pallas_call | solution.py:49
  70.6 3.1 %collective-permute-start.20 = (bf16[272,128]{1,0:T(8,128)(2,1)S(1)}, bf16[272,128]{1,0:T(8,128)(2,1)S(1)}, u32[]{:S(2)}, u32[]{:S(2)}) collective-permute-start(bf16[272,128]{1,0:T(8,128)(2,1)S(1)} %get-tuple-element.137.refs_4_), channel_id=1, source_target_pairs={{0,64},{32,96},{64,0},{96,32},{1,65},{33,97},{65,1},{97,33},{2,66}... | collective-permute-start | bytes 208904 | tf_op jit(solution)/shard_map/ppermute | solution.py:645
  74.0 2.7 %collective-permute-done.20.refs_6_ = bf16[272,128]{1,0:T(8,128)(2,1)S(1)} collective-permute-done((bf16[272,128]{1,0:T(8,128)(2,1)S(1)}, bf16[272,128]{1,0:T(8,128)(2,1)S(1)}, u32[]{:S(2)}, u32[]{:S(2)}) %collective-permute-start.20) | collective-permute-done | bytes 69664 | tf_op jit(solution)/shard_map/ppermute | solution.py:645
  76.7 2.6 %collective-permute-done.21.refs_7_ = bf16[272,128]{1,0:T(8,128)(2,1)S(1)} collective-permute-done((bf16[272,128]{1,0:T(8,128)(2,1)S(1)}, bf16[272,128]{1,0:T(8,128)(2,1)S(1)}, u32[]{:S(2)}, u32[]{:S(2)}) %collective-permute-start.21) | collective-permute-done | bytes 69664 | tf_op jit(solution)/shard_map/ppermute | solution.py:645
  79.3 3.7 %shard_map.100 = (bf16[256,1536]{1,0:T(8,128)(2,1)S(1)}, bf16[256,128]{1,0:T(8,128)(2,1)S(1)}, bf16[256,128]{1,0:T(8,128)(2,1)S(1)}, bf16[256,1536]{1,0:T(8,128)(2,1)S(1)}, f32[256,128]{1,0:T(8,128)S(1)}) custom-call(s32[2,1]{1,0:T(2,128)S(1)} %copy.24.ids, bf16[272,128]{1,0:T(8,128)(2,1)S(1)} %shard_map.96.refs_0_, ...), custom_call_target="tpu_custom_call" | custom-call | flops 100000000 | bytes 4000000 | tf_op jit(solution)/shard_map/pallas_call | solution.py:49
  84.8 1.7 collective-permute-start.24
  86.4 2.6 %collective-permute-done.23.refs_2_ = bf16[256,128]{1,0:T(8,128)(2,1)S(1)} collective-permute-done((bf16[256,128]{1,0:T(8,128)(2,1)S(1)}, bf16[256,128]{1,0:T(8,128)(2,1)S(1)}, u32[]{:S(2)}, u32[]{:S(2)}) %collective-permute-start.23) | collective-permute-done | bytes 65568 | tf_op jit(solution)/shard_map/ppermute | solution.py:645
  90.5 3.2 %shard_map.101 = (bf16[256,1536]{1,0:T(8,128)(2,1)S(1)}, bf16[256,128]{1,0:T(8,128)(2,1)S(1)}, bf16[256,128]{1,0:T(8,128)(2,1)S(1)}) custom-call(s32[2,1]{1,0:T(2,128)S(1)} %copy.24.ids, bf16[256,128]{1,0:T(8,128)(2,1)S(1)} %get-tuple-element.141.refs_0_, bf16[256,128]{1,0:T(8,128)(2,1)S(1)} %collective-permute-done.22.refs_1_, ...), custom_call_target="tpu_custom_call" | custom-call | flops 100000000 | bytes 4000000 | tf_op jit(solution)/shard_map/pallas_call | solution.py:49
  94.0 1.9 collective-permute-start.26
  97.2 2.1 %shard_map.103 = (bf16[1536,128]{1,0:T(8,128)(2,1)S(1)}, bf16[128,1536]{1,0:T(8,128)(2,1)S(1)}) custom-call(s32[2,1]{1,0:T(2,128)S(1)} %copy.24.ids, bf16[256,1536]{1,0:T(8,128)(2,1)S(1)} %get-tuple-element.152.refs_0_, f32[256,128]{1,0:T(8,128)S(1)} %get-tuple-element.153.refs_1_, bf16[2,128,6144]{2,1,0:T(8,128)(2,1)} %refs_2_.5, ...), custom_call_target="tpu_custom_call" | custom-call | flops 100000000 | bytes 4000000 | tf_op jit(solution)/shard_map/pallas_call | solution.py:49
  101.4 3.2 %shard_map.104 = (bf16[256,1536]{1,0:T(8,128)(2,1)S(1)}, bf16[256,128]{1,0:T(8,128)(2,1)S(1)}, bf16[256,128]{1,0:T(8,128)(2,1)S(1)}) custom-call(s32[2,1]{1,0:T(2,128)S(1)} %copy.24.ids, bf16[256,128]{1,0:T(8,128)(2,1)S(1)} %get-tuple-element.158.refs_0_, bf16[256,128]{1,0:T(8,128)(2,1)S(1)} %collective-permute-done.25.refs_1_, ...), custom_call_target="tpu_custom_call" | custom-call | flops 100000000 | bytes 4000000 | tf_op jit(solution)/shard_map/pallas_call | solution.py:49
  108.6 2.1 %collective-permute-done.29.refs_2_ = bf16[256,128]{1,0:T(8,128)(2,1)S(1)} collective-permute-done((bf16[256,128]{1,0:T(8,128)(2,1)S(1)}, bf16[256,128]{1,0:T(8,128)(2,1)S(1)}, u32[]{:S(2)}, u32[]{:S(2)}) %collective-permute-start.29) | collective-permute-done | bytes 65568 | tf_op jit(solution)/shard_map/ppermute | solution.py:645
  117.4 2.5 %collective-permute-start.34 = (bf16[2,32,1536]{2,1,0:T(8,128)(2,1)S(1)}, bf16[2,32,1536]{2,1,0:T(8,128)(2,1)S(1)}, u32[]{:S(2)}, u32[]{:S(2)}) collective-permute-start(bf16[2,32,1536]{2,1,0:T(8,128)(2,1)S(1)} %get-tuple-element.188), channel_id=1, source_target_pairs={{0,3},{1,0},{2,1},{3,2},{4,7},{5,4},{6,5},{7,6},{8,11},{9,8},{10,9... | collective-permute-start | bytes 589832 | tf_op jit(solution)/shard_map/ppermute | solution.py:583
  121.7 2.6 %collective-permute-done.33.b_lo = bf16[2,32,1536]{2,1,0:T(8,128)(2,1)S(1)} collective-permute-done((bf16[2,32,1536]{2,1,0:T(8,128)(2,1)S(1)}, bf16[2,32,1536]{2,1,0:T(8,128)(2,1)S(1)}, u32[]{:S(2)}, u32[]{:S(2)}) %collective-permute-start.33) | collective-permute-done | bytes 196640 | tf_op jit(solution)/shard_map/ppermute | solution.py:583
  124.9 2.9 %collective-permute-start.36 = (bf16[4,384,128]{2,1,0:T(8,128)(2,1)S(1)}, bf16[4,384,128]{2,1,0:T(8,128)(2,1)S(1)}, u32[]{:S(2)}, u32[]{:S(2)}) collective-permute-start(bf16[4,384,128]{2,1,0:T(8,128)(2,1)S(1)} %get-tuple-element.190), channel_id=1, source_target_pairs={{0,24},{1,25},{2,26},{3,27},{4,28},{5,29},{6,30},{7,31},{8,0},{9,1... | collective-permute-start | bytes 1179656 | tf_op jit(solution)/shard_map/ppermute | solution.py:579
  129.2 1.9 collective-permute-start.38
  131.0 4.4 %collective-permute-done.35.refs_1_ = bf16[4,384,128]{2,1,0:T(8,128)(2,1)S(1)} collective-permute-done((bf16[4,384,128]{2,1,0:T(8,128)(2,1)S(1)}, bf16[4,384,128]{2,1,0:T(8,128)(2,1)S(1)}, u32[]{:S(2)}, u32[]{:S(2)}) %collective-permute-start.35) | collective-permute-done | bytes 393248 | tf_op jit(solution)/shard_map/ppermute | solution.py:579
  135.4 2.7 %collective-permute-done.37.refs_4_ = bf16[4,32,1536]{2,1,0:T(8,128)(2,1)S(1)} collective-permute-done((bf16[4,32,1536]{2,1,0:T(8,128)(2,1)S(1)}, bf16[4,32,1536]{2,1,0:T(8,128)(2,1)S(1)}, u32[]{:S(2)}, u32[]{:S(2)}) %collective-permute-start.37) | collective-permute-done | bytes 393248 | tf_op jit(solution)/shard_map/ppermute | solution.py:583
  140.0 3.6 %collective-permute-start.40 = (bf16[4,96,128]{2,1,0:T(8,128)(2,1)S(1)}, bf16[4,96,128]{2,1,0:T(8,128)(2,1)S(1)}, u32[]{:S(2)}, u32[]{:S(2)}) collective-permute-start(bf16[4,96,128]{2,1,0:T(8,128)(2,1)S(1)} %get-tuple-element.196), channel_id=1, source_target_pairs={{0,2},{1,3},{2,0},{3,1},{4,6},{5,7},{6,4},{7,5},{8,10},{9,11},{10,... | collective-permute-start | bytes 294920 | tf_op jit(solution)/shard_map/ppermute | solution.py:583
  144.4 1.8 collective-permute-start.43
  148.2 3.1 %collective-permute-done.42.b1 = bf16[4,32,384]{2,1,0:T(8,128)(2,1)S(1)} collective-permute-done((bf16[4,32,384]{2,1,0:T(8,128)(2,1)S(1)}, bf16[4,32,384]{2,1,0:T(8,128)(2,1)S(1)}, u32[]{:S(2)}, u32[]{:S(2)}) %collective-permute-start.42) | collective-permute-done | bytes 98336 | tf_op jit(solution)/shard_map/ppermute | solution.py:579
  152.3 1.7 collective-permute-start.45
  154.0 4.0 %collective-permute-done.45 = bf16[4,192,128]{2,1,0:T(8,128)(2,1)S(1)} collective-permute-done((bf16[4,192,128]{2,1,0:T(8,128)(2,1)S(1)}, bf16[4,192,128]{2,1,0:T(8,128)(2,1)S(1)}, u32[]{:S(2)}, u32[]{:S(2)}) %collective-permute-start.45) | collective-permute-done | bytes 196640 | tf_op jit(solution)/shard_map/ppermute | solution.py:587
  158.3 2.0 collective-permute-start.47
  161.6 2.3 %collective-permute-done.47 = bf16[192,128]{1,0:T(8,128)(2,1)S(1)} collective-permute-done((bf16[192,128]{1,0:T(8,128)(2,1)S(1)}, bf16[192,128]{1,0:T(8,128)(2,1)S(1)}, u32[]{:S(2)}, u32[]{:S(2)}) %collective-permute-start.47) | collective-permute-done | bytes 49184 | tf_op jit(solution)/shard_map/ppermute | solution.py:645
  166.5 2.9 %collective-permute-start.57 = (bf16[4,96,128]{2,1,0:T(8,128)(2,1)S(1)}, bf16[4,96,128]{2,1,0:T(8,128)(2,1)S(1)}, u32[]{:S(2)}, u32[]{:S(2)}) collective-permute-start(bf16[4,96,128]{2,1,0:T(8,128)(2,1)S(1)} %get-tuple-element.208), channel_id=1, source_target_pairs={{0,16},{1,17},{2,18},{3,19},{4,20},{5,21},{6,22},{7,23},{8,24},{9,... | collective-permute-start | bytes 294920 | tf_op jit(solution)/shard_map/ppermute | solution.py:579
  170.3 3.0 %collective-permute-start.51 = (bf16[4,96,128]{2,1,0:T(8,128)(2,1)S(1)}, bf16[4,96,128]{2,1,0:T(8,128)(2,1)S(1)}, u32[]{:S(2)}, u32[]{:S(2)}) collective-permute-start(bf16[4,96,128]{2,1,0:T(8,128)(2,1)S(1)} %get-tuple-element.209), channel_id=1, source_target_pairs={{0,3},{1,0},{2,1},{3,2},{4,7},{5,4},{6,5},{7,6},{8,11},{9,8},{10,9... | collective-permute-start | bytes 294920 | tf_op jit(solution)/shard_map/ppermute | solution.py:583
  175.7 2.1 %collective-permute-start.61 = (bf16[4,4,96,128]{3,2,1,0:T(8,128)(2,1)S(1)}, bf16[4,4,96,128]{3,2,1,0:T(8,128)(2,1)S(1)}, u32[]{:S(2)}, u32[]{:S(2)}) collective-permute-start(bf16[4,4,96,128]{3,2,1,0:T(8,128)(2,1)S(1)} %pad_maximum_fusion.3.refs_3_), channel_id=1, source_target_pairs={{0,3},{1,0},{2,1},{3,2},{4,7},{5,4},{6,5},{7,6},{8,11},{9,8},{10,9... | collective-permute-start | bytes 1179656 | tf_op jit(solution)/shard_map/ppermute | solution.py:583
  177.8 2.3 %collective-permute-done.49 = bf16[4,96,128]{2,1,0:T(8,128)(2,1)S(1)} collective-permute-done((bf16[4,96,128]{2,1,0:T(8,128)(2,1)S(1)}, bf16[4,96,128]{2,1,0:T(8,128)(2,1)S(1)}, u32[]{:S(2)}, u32[]{:S(2)}) %collective-permute-start.49) | collective-permute-done | bytes 98336 | tf_op jit(solution)/shard_map/ppermute | solution.py:583
  180.1 2.2 %collective-permute-start.52 = (bf16[4,4,96,128]{3,2,1,0:T(8,128)(2,1)S(1)}, bf16[4,4,96,128]{3,2,1,0:T(8,128)(2,1)S(1)}, u32[]{:S(2)}, u32[]{:S(2)}) collective-permute-start(bf16[4,4,96,128]{3,2,1,0:T(8,128)(2,1)S(1)} %pad_maximum_fusion.2.refs_0_), channel_id=1, source_target_pairs={{0,8},{1,9},{2,10},{3,11},{4,12},{5,13},{6,14},{7,15},{8,16},{9,17... | collective-permute-start | bytes 1179656 | tf_op jit(solution)/shard_map/ppermute | solution.py:579
  183.4 3.7 %collective-permute-done.59.refs_4_ = bf16[4,4,96,128]{3,2,1,0:T(8,128)(2,1)S(1)} collective-permute-done((bf16[4,4,96,128]{3,2,1,0:T(8,128)(2,1)S(1)}, bf16[4,4,96,128]{3,2,1,0:T(8,128)(2,1)S(1)}, u32[]{:S(2)}, u32[]{:S(2)}) %collective-permute-start.59) | collective-permute-done | bytes 393248 | tf_op jit(solution)/shard_map/ppermute | solution.py:583
  187.3 3.3 %collective-permute-start.62 = (bf16[2,4,96,128]{3,2,1,0:T(8,128)(2,1)S(1)}, bf16[2,4,96,128]{3,2,1,0:T(8,128)(2,1)S(1)}, u32[]{:S(2)}, u32[]{:S(2)}) collective-permute-start(bf16[2,4,96,128]{3,2,1,0:T(8,128)(2,1)S(1)} %slice.37), channel_id=1, source_target_pairs={{0,3},{1,0},{2,1},{3,2},{4,7},{5,4},{6,5},{7,6},{8,11},{9,8},{10,9... | collective-permute-start | bytes 589832 | tf_op jit(solution)/shard_map/ppermute | solution.py:583
  190.6 1.7 collective-permute-start.53
  192.3 1.7 collective-permute-start.55
  194.0 2.4 %shard_map.110 = (bf16[1,1,6144,128]{3,2,1,0:T(8,128)(2,1)}, bf16[1,1,128,6144]{3,2,1,0:T(8,128)(2,1)}) custom-call(s32[2,1]{1,0:T(2,128)S(1)} %copy.24.ids, bf16[4,4,96,128]{3,2,1,0:T(8,128)(2,1)S(1)} %pad_maximum_fusion.2.refs_0_, bf16[4,4,96,128]{3,2,1,0:T(8,128)(2,1)S(1)} %collective-permute-done.52.refs_1_, ...), custom_call_target="tpu_custom_call" | custom-call | flops 100000000 | bytes 4000000 | tf_op jit(solution)/shard_map/pallas_call | solution.py:49
  (109 shorter events, 58.5 us)
Async XLA Ops:
  3.9 10.9 %collective-permute-start = (bf16[1536,128]{1,0:T(8,128)(2,1)S(1)}, bf16[1536,128]{1,0:T(8,128)(2,1)S(1)}, u32[]{:S(2)}, u32[]{:S(2)}) collective-permute-start(bf16[1536,128]{1,0:T(8,128)(2,1)S(1)} %get-tuple-element.103), channel_id=1, source_target_pairs={{0,68},{1,69},{2,70},{3,71},{4,64},{5,65},{6,66},{7,67},{8,76},{9,... | collective-permute-start | bytes 1179656 | tf_op jit(solution)/shard_map/ppermute | solution.py:652
  14.8 5.8 %collective-permute-start.1 = (bf16[768,128]{1,0:T(8,128)(2,1)S(1)}, bf16[768,128]{1,0:T(8,128)(2,1)S(1)}, u32[]{:S(2)}, u32[]{:S(2)}) collective-permute-start(bf16[768,128]{1,0:T(8,128)(2,1)S(1)} %get-tuple-element.205), channel_id=1, source_target_pairs={{0,8},{1,9},{2,10},{3,11},{4,12},{5,13},{6,14},{7,15},{8,0},{9,1},... | collective-permute-start | bytes 589832 | tf_op jit(solution)/shard_map/ppermute | solution.py:656
  16.4 19.6 %collective-permute-start.8 = (bf16[256,1536]{1,0:T(8,128)(2,1)S(1)}, bf16[256,1536]{1,0:T(8,128)(2,1)S(1)}, u32[]{:S(2)}, u32[]{:S(2)}) collective-permute-start(bf16[256,1536]{1,0:T(8,128)(2,1)S(1)} %get-tuple-element.117), channel_id=1, source_target_pairs={{0,64},{32,96},{64,0},{96,32},{1,65},{33,97},{65,1},{97,33},{2,66}... | collective-permute-start | bytes 2359304 | tf_op jit(solution)/shard_map/ppermute | solution.py:645
  18.4 6.6 %collective-permute-start.3 = (bf16[768,128]{1,0:T(8,128)(2,1)S(1)}, bf16[768,128]{1,0:T(8,128)(2,1)S(1)}, u32[]{:S(2)}, u32[]{:S(2)}) collective-permute-start(bf16[768,128]{1,0:T(8,128)(2,1)S(1)} %get-tuple-element.204), channel_id=1, source_target_pairs={{0,33},{1,32},{2,35},{3,34},{4,37},{5,36},{6,39},{7,38},{8,41},{9,... | collective-permute-start | bytes 589832 | tf_op jit(solution)/shard_map/ppermute | solution.py:656
  25.9 11.5 %collective-permute-start.6 = (bf16[1536,128]{1,0:T(8,128)(2,1)S(1)}, bf16[1536,128]{1,0:T(8,128)(2,1)S(1)}, u32[]{:S(2)}, u32[]{:S(2)}) collective-permute-start(bf16[1536,128]{1,0:T(8,128)(2,1)S(1)} %pad_maximum_fusion.refs_12_), channel_id=1, source_target_pairs={{0,1},{1,0},{2,3},{3,2},{4,5},{5,4},{6,7},{7,6},{8,9},{9,8},{10,11... | collective-permute-start | bytes 1179656 | tf_op jit(solution)/shard_map/ppermute | solution.py:656
  27.5 11.2 %collective-permute-start.7 = (bf16[1536,128]{1,0:T(8,128)(2,1)S(1)}, bf16[1536,128]{1,0:T(8,128)(2,1)S(1)}, u32[]{:S(2)}, u32[]{:S(2)}) collective-permute-start(bf16[1536,128]{1,0:T(8,128)(2,1)S(1)} %pad_maximum_fusion.1.refs_14_), channel_id=1, source_target_pairs={{0,8},{1,9},{2,10},{3,11},{4,12},{5,13},{6,14},{7,15},{8,0},{9,1},... | collective-permute-start | bytes 1179656 | tf_op jit(solution)/shard_map/ppermute | solution.py:656
  29.3 9.3 %collective-permute-start.10 = (bf16[272,128]{1,0:T(8,128)(2,1)S(1)}, bf16[272,128]{1,0:T(8,128)(2,1)S(1)}, u32[]{:S(2)}, u32[]{:S(2)}) collective-permute-start(bf16[272,128]{1,0:T(8,128)(2,1)S(1)} %shard_map.96.refs_0_), channel_id=1, source_target_pairs={{0,64},{96,32},{1,65},{97,33},{2,66},{98,34},{3,67},{99,35},{4,68}... | collective-permute-start | bytes 208904 | tf_op jit(solution)/shard_map/ppermute | solution.py:645
  31.1 7.5 %collective-permute-start.11 = (bf16[272,128]{1,0:T(8,128)(2,1)S(1)}, bf16[272,128]{1,0:T(8,128)(2,1)S(1)}, u32[]{:S(2)}, u32[]{:S(2)}) collective-permute-start(bf16[272,128]{1,0:T(8,128)(2,1)S(1)} %shard_map.96.refs_0_), channel_id=1, source_target_pairs={{0,96},{96,0},{1,97},{97,1},{2,98},{98,2},{3,99},{99,3},{4,100},{1... | collective-permute-start | bytes 208904 | tf_op jit(solution)/shard_map/ppermute | solution.py:645
  43.3 11.4 %collective-permute-start.15 = (bf16[256,1536]{1,0:T(8,128)(2,1)S(1)}, bf16[256,1536]{1,0:T(8,128)(2,1)S(1)}, u32[]{:S(2)}, u32[]{:S(2)}) collective-permute-start(bf16[256,1536]{1,0:T(8,128)(2,1)S(1)} %get-tuple-element.134), channel_id=1, source_target_pairs={{32,0},{64,96},{33,1},{65,97},{34,2},{66,98},{35,3},{67,99},{36,4}... | collective-permute-start | bytes 2359304 | tf_op jit(solution)/shard_map/ppermute | solution.py:645
  46.3 6.1 %collective-permute-start.13 = (bf16[272,128]{1,0:T(8,128)(2,1)S(1)}, bf16[272,128]{1,0:T(8,128)(2,1)S(1)}, u32[]{:S(2)}, u32[]{:S(2)}) collective-permute-start(bf16[272,128]{1,0:T(8,128)(2,1)S(1)} %get-tuple-element.132.refs_0_), channel_id=1, source_target_pairs={{0,64},{32,96},{64,0},{96,32},{1,65},{33,97},{65,1},{97,33},{2,66}... | collective-permute-start | bytes 208904 | tf_op jit(solution)/shard_map/ppermute | solution.py:645
  48.7 6.0 %collective-permute-start.14 = (bf16[272,128]{1,0:T(8,128)(2,1)S(1)}, bf16[272,128]{1,0:T(8,128)(2,1)S(1)}, u32[]{:S(2)}, u32[]{:S(2)}) collective-permute-start(bf16[272,128]{1,0:T(8,128)(2,1)S(1)} %get-tuple-element.132.refs_0_), channel_id=1, source_target_pairs={{0,96},{32,64},{64,32},{96,0},{1,97},{33,65},{65,33},{97,1},{2,98}... | collective-permute-start | bytes 208904 | tf_op jit(solution)/shard_map/ppermute | solution.py:645
  59.2 5.8 %collective-permute-start.17 = (bf16[272,128]{1,0:T(8,128)(2,1)S(1)}, bf16[272,128]{1,0:T(8,128)(2,1)S(1)}, u32[]{:S(2)}, u32[]{:S(2)}) collective-permute-start(bf16[272,128]{1,0:T(8,128)(2,1)S(1)} %get-tuple-element.135.refs_0_), channel_id=1, source_target_pairs={{0,64},{32,96},{64,0},{96,32},{1,65},{33,97},{65,1},{97,33},{2,66}... | collective-permute-start | bytes 208904 | tf_op jit(solution)/shard_map/ppermute | solution.py:645
  60.6 5.7 %collective-permute-start.18 = (bf16[272,128]{1,0:T(8,128)(2,1)S(1)}, bf16[272,128]{1,0:T(8,128)(2,1)S(1)}, u32[]{:S(2)}, u32[]{:S(2)}) collective-permute-start(bf16[272,128]{1,0:T(8,128)(2,1)S(1)} %get-tuple-element.135.refs_0_), channel_id=1, source_target_pairs={{0,96},{32,64},{64,32},{96,0},{1,97},{33,65},{65,33},{97,1},{2,98}... | collective-permute-start | bytes 208904 | tf_op jit(solution)/shard_map/ppermute | solution.py:645
  70.6 6.1 %collective-permute-start.20 = (bf16[272,128]{1,0:T(8,128)(2,1)S(1)}, bf16[272,128]{1,0:T(8,128)(2,1)S(1)}, u32[]{:S(2)}, u32[]{:S(2)}) collective-permute-start(bf16[272,128]{1,0:T(8,128)(2,1)S(1)} %get-tuple-element.137.refs_4_), channel_id=1, source_target_pairs={{0,64},{32,96},{64,0},{96,32},{1,65},{33,97},{65,1},{97,33},{2,66}... | collective-permute-start | bytes 208904 | tf_op jit(solution)/shard_map/ppermute | solution.py:645
  73.7 5.7 %collective-permute-start.21 = (bf16[272,128]{1,0:T(8,128)(2,1)S(1)}, bf16[272,128]{1,0:T(8,128)(2,1)S(1)}, u32[]{:S(2)}, u32[]{:S(2)}) collective-permute-start(bf16[272,128]{1,0:T(8,128)(2,1)S(1)} %get-tuple-element.137.refs_4_), channel_id=1, source_target_pairs={{0,96},{32,64},{64,32},{96,0},{1,97},{33,65},{65,33},{97,1},{2,98}... | collective-permute-start | bytes 208904 | tf_op jit(solution)/shard_map/ppermute | solution.py:645
  83.2 5.9 %collective-permute-start.23 = (bf16[256,128]{1,0:T(8,128)(2,1)S(1)}, bf16[256,128]{1,0:T(8,128)(2,1)S(1)}, u32[]{:S(2)}, u32[]{:S(2)}) collective-permute-start(bf16[256,128]{1,0:T(8,128)(2,1)S(1)} %get-tuple-element.141.refs_0_), channel_id=1, source_target_pairs={{0,64},{32,96},{64,0},{96,32},{1,65},{33,97},{65,1},{97,33},{2,66}... | collective-permute-start | bytes 196616 | tf_op jit(solution)/shard_map/ppermute | solution.py:645
  84.8 5.8 %collective-permute-start.24 = (bf16[256,128]{1,0:T(8,128)(2,1)S(1)}, bf16[256,128]{1,0:T(8,128)(2,1)S(1)}, u32[]{:S(2)}, u32[]{:S(2)}) collective-permute-start(bf16[256,128]{1,0:T(8,128)(2,1)S(1)} %get-tuple-element.141.refs_0_), channel_id=1, source_target_pairs={{0,96},{32,64},{64,32},{96,0},{1,97},{33,65},{65,33},{97,1},{2,98}... | collective-permute-start | bytes 196616 | tf_op jit(solution)/shard_map/ppermute | solution.py:645
  93.8 6.1 %collective-permute-start.25 = (bf16[256,128]{1,0:T(8,128)(2,1)S(1)}, bf16[256,128]{1,0:T(8,128)(2,1)S(1)}, u32[]{:S(2)}, u32[]{:S(2)}) collective-permute-start(bf16[256,128]{1,0:T(8,128)(2,1)S(1)} %get-tuple-element.158.refs_0_), channel_id=1, source_target_pairs={{0,32},{32,0},{64,96},{96,64},{1,33},{33,1},{65,97},{97,65},{2,34}... | collective-permute-start | bytes 196616 | tf_op jit(solution)/shard_map/ppermute | solution.py:645
  94.0 5.9 %collective-permute-start.26 = (bf16[256,128]{1,0:T(8,128)(2,1)S(1)}, bf16[256,128]{1,0:T(8,128)(2,1)S(1)}, u32[]{:S(2)}, u32[]{:S(2)}) collective-permute-start(bf16[256,128]{1,0:T(8,128)(2,1)S(1)} %get-tuple-element.158.refs_0_), channel_id=1, source_target_pairs={{0,64},{32,96},{64,0},{96,32},{1,65},{33,97},{65,1},{97,33},{2,66}... | collective-permute-start | bytes 196616 | tf_op jit(solution)/shard_map/ppermute | solution.py:645
  104.9 5.9 %collective-permute-start.29 = (bf16[256,128]{1,0:T(8,128)(2,1)S(1)}, bf16[256,128]{1,0:T(8,128)(2,1)S(1)}, u32[]{:S(2)}, u32[]{:S(2)}) collective-permute-start(bf16[256,128]{1,0:T(8,128)(2,1)S(1)} %get-tuple-element.169.refs_0_), channel_id=1, source_target_pairs={{0,64},{32,96},{64,0},{96,32},{1,65},{33,97},{65,1},{97,33},{2,66}... | collective-permute-start | bytes 196616 | tf_op jit(solution)/shard_map/ppermute | solution.py:645
  113.4 8.2 %collective-permute-start.31 = (bf16[2,384,128]{2,1,0:T(8,128)(2,1)S(1)}, bf16[2,384,128]{2,1,0:T(8,128)(2,1)S(1)}, u32[]{:S(2)}, u32[]{:S(2)}) collective-permute-start(bf16[2,384,128]{2,1,0:T(8,128)(2,1)S(1)} %get-tuple-element.183), channel_id=1, source_target_pairs={{0,8},{1,9},{2,10},{3,11},{4,12},{5,13},{6,14},{7,15},{8,16},{9,17... | collective-permute-start | bytes 589832 | tf_op jit(solution)/shard_map/ppermute | solution.py:579
  115.0 6.6 %collective-permute-start.32 = (bf16[2,384,128]{2,1,0:T(8,128)(2,1)S(1)}, bf16[2,384,128]{2,1,0:T(8,128)(2,1)S(1)}, u32[]{:S(2)}, u32[]{:S(2)}) collective-permute-start(bf16[2,384,128]{2,1,0:T(8,128)(2,1)S(1)} %get-tuple-element.184), channel_id=1, source_target_pairs={{0,24},{1,25},{2,26},{3,27},{4,28},{5,29},{6,30},{7,31},{8,0},{9,1... | collective-permute-start | bytes 589832 | tf_op jit(solution)/shard_map/ppermute | solution.py:579
  116.7 7.6 %collective-permute-start.33 = (bf16[2,32,1536]{2,1,0:T(8,128)(2,1)S(1)}, bf16[2,32,1536]{2,1,0:T(8,128)(2,1)S(1)}, u32[]{:S(2)}, u32[]{:S(2)}) collective-permute-start(bf16[2,32,1536]{2,1,0:T(8,128)(2,1)S(1)} %get-tuple-element.187), channel_id=1, source_target_pairs={{0,1},{1,2},{2,3},{3,0},{4,5},{5,6},{6,7},{7,4},{8,9},{9,10},{10,1... | collective-permute-start | bytes 589832 | tf_op jit(solution)/shard_map/ppermute | solution.py:583
  117.4 6.9 %collective-permute-start.34 = (bf16[2,32,1536]{2,1,0:T(8,128)(2,1)S(1)}, bf16[2,32,1536]{2,1,0:T(8,128)(2,1)S(1)}, u32[]{:S(2)}, u32[]{:S(2)}) collective-permute-start(bf16[2,32,1536]{2,1,0:T(8,128)(2,1)S(1)} %get-tuple-element.188), channel_id=1, source_target_pairs={{0,3},{1,0},{2,1},{3,2},{4,7},{5,4},{6,5},{7,6},{8,11},{9,8},{10,9... | collective-permute-start | bytes 589832 | tf_op jit(solution)/shard_map/ppermute | solution.py:583
  124.5 10.9 %collective-permute-start.35 = (bf16[4,384,128]{2,1,0:T(8,128)(2,1)S(1)}, bf16[4,384,128]{2,1,0:T(8,128)(2,1)S(1)}, u32[]{:S(2)}, u32[]{:S(2)}) collective-permute-start(bf16[4,384,128]{2,1,0:T(8,128)(2,1)S(1)} %get-tuple-element.189), channel_id=1, source_target_pairs={{0,8},{1,9},{2,10},{3,11},{4,12},{5,13},{6,14},{7,15},{8,16},{9,17... | collective-permute-start | bytes 1179656 | tf_op jit(solution)/shard_map/ppermute | solution.py:579
  124.9 10.5 %collective-permute-start.36 = (bf16[4,384,128]{2,1,0:T(8,128)(2,1)S(1)}, bf16[4,384,128]{2,1,0:T(8,128)(2,1)S(1)}, u32[]{:S(2)}, u32[]{:S(2)}) collective-permute-start(bf16[4,384,128]{2,1,0:T(8,128)(2,1)S(1)} %get-tuple-element.190), channel_id=1, source_target_pairs={{0,24},{1,25},{2,26},{3,27},{4,28},{5,29},{6,30},{7,31},{8,0},{9,1... | collective-permute-start | bytes 1179656 | tf_op jit(solution)/shard_map/ppermute | solution.py:579
  127.8 10.3 %collective-permute-start.37 = (bf16[4,32,1536]{2,1,0:T(8,128)(2,1)S(1)}, bf16[4,32,1536]{2,1,0:T(8,128)(2,1)S(1)}, u32[]{:S(2)}, u32[]{:S(2)}) collective-permute-start(bf16[4,32,1536]{2,1,0:T(8,128)(2,1)S(1)} %get-tuple-element.192), channel_id=1, source_target_pairs={{0,1},{1,2},{2,3},{3,0},{4,5},{5,6},{6,7},{7,4},{8,9},{9,10},{10,1... | collective-permute-start | bytes 1179656 | tf_op jit(solution)/shard_map/ppermute | solution.py:583
  129.2 9.0 %collective-permute-start.38 = (bf16[4,32,1536]{2,1,0:T(8,128)(2,1)S(1)}, bf16[4,32,1536]{2,1,0:T(8,128)(2,1)S(1)}, u32[]{:S(2)}, u32[]{:S(2)}) collective-permute-start(bf16[4,32,1536]{2,1,0:T(8,128)(2,1)S(1)} %get-tuple-element.193), channel_id=1, source_target_pairs={{0,3},{1,0},{2,1},{3,2},{4,7},{5,4},{6,5},{7,6},{8,11},{9,8},{10,9... | collective-permute-start | bytes 1179656 | tf_op jit(solution)/shard_map/ppermute | solution.py:583
  139.1 7.1 %collective-permute-start.39 = (bf16[4,96,128]{2,1,0:T(8,128)(2,1)S(1)}, bf16[4,96,128]{2,1,0:T(8,128)(2,1)S(1)}, u32[]{:S(2)}, u32[]{:S(2)}) collective-permute-start(bf16[4,96,128]{2,1,0:T(8,128)(2,1)S(1)} %get-tuple-element.195), channel_id=1, source_target_pairs={{0,1},{1,2},{2,3},{3,0},{4,5},{5,6},{6,7},{7,4},{8,9},{9,10},{10,1... | collective-permute-start | bytes 294920 | tf_op jit(solution)/shard_map/ppermute | solution.py:583
  140.0 7.7 %collective-permute-start.40 = (bf16[4,96,128]{2,1,0:T(8,128)(2,1)S(1)}, bf16[4,96,128]{2,1,0:T(8,128)(2,1)S(1)}, u32[]{:S(2)}, u32[]{:S(2)}) collective-permute-start(bf16[4,96,128]{2,1,0:T(8,128)(2,1)S(1)} %get-tuple-element.196), channel_id=1, source_target_pairs={{0,2},{1,3},{2,0},{3,1},{4,6},{5,7},{6,4},{7,5},{8,10},{9,11},{10,... | collective-permute-start | bytes 294920 | tf_op jit(solution)/shard_map/ppermute | solution.py:583
  144.4 6.9 %collective-permute-start.42 = (bf16[4,32,384]{2,1,0:T(8,128)(2,1)S(1)}, bf16[4,32,384]{2,1,0:T(8,128)(2,1)S(1)}, u32[]{:S(2)}, u32[]{:S(2)}) collective-permute-start(bf16[4,32,384]{2,1,0:T(8,128)(2,1)S(1)} %get-tuple-element.199), channel_id=1, source_target_pairs={{0,8},{1,9},{2,10},{3,11},{4,12},{5,13},{6,14},{7,15},{8,16},{9,17... | collective-permute-start | bytes 294920 | tf_op jit(solution)/shard_map/ppermute | solution.py:579
  144.4 6.9 %collective-permute-start.43 = (bf16[4,32,384]{2,1,0:T(8,128)(2,1)S(1)}, bf16[4,32,384]{2,1,0:T(8,128)(2,1)S(1)}, u32[]{:S(2)}, u32[]{:S(2)}) collective-permute-start(bf16[4,32,384]{2,1,0:T(8,128)(2,1)S(1)} %get-tuple-element.200), channel_id=1, source_target_pairs={{0,16},{1,17},{2,18},{3,19},{4,20},{5,21},{6,22},{7,23},{8,24},{9,... | collective-permute-start | bytes 294920 | tf_op jit(solution)/shard_map/ppermute | solution.py:579
  146.2 6.0 %collective-permute-start.44 = (bf16[4,32,384]{2,1,0:T(8,128)(2,1)S(1)}, bf16[4,32,384]{2,1,0:T(8,128)(2,1)S(1)}, u32[]{:S(2)}, u32[]{:S(2)}) collective-permute-start(bf16[4,32,384]{2,1,0:T(8,128)(2,1)S(1)} %get-tuple-element.201), channel_id=1, source_target_pairs={{0,24},{1,25},{2,26},{3,27},{4,28},{5,29},{6,30},{7,31},{8,0},{9,1... | collective-permute-start | bytes 294920 | tf_op jit(solution)/shard_map/ppermute | solution.py:579
  152.3 5.8 %collective-permute-start.45 = (bf16[4,192,128]{2,1,0:T(8,128)(2,1)S(1)}, bf16[4,192,128]{2,1,0:T(8,128)(2,1)S(1)}, u32[]{:S(2)}, u32[]{:S(2)}) collective-permute-start(bf16[4,192,128]{2,1,0:T(8,128)(2,1)S(1)} %shard_map.109), channel_id=1, source_target_pairs={{0,4},{1,5},{2,6},{3,7},{4,0},{5,1},{6,2},{7,3},{8,12},{9,13},{10,... | collective-permute-start | bytes 589832 | tf_op jit(solution)/shard_map/ppermute | solution.py:587
  158.3 5.7 %collective-permute-start.47 = (bf16[192,128]{1,0:T(8,128)(2,1)S(1)}, bf16[192,128]{1,0:T(8,128)(2,1)S(1)}, u32[]{:S(2)}, u32[]{:S(2)}) collective-permute-start(bf16[192,128]{1,0:T(8,128)(2,1)S(1)} %get-tuple-element.212), channel_id=1, source_target_pairs={{0,64},{32,96},{64,0},{96,32},{1,65},{33,97},{65,1},{97,33},{2,66}... | collective-permute-start | bytes 147464 | tf_op jit(solution)/shard_map/ppermute | solution.py:645
  165.5 7.7 %collective-permute-start.56 = (bf16[4,96,128]{2,1,0:T(8,128)(2,1)S(1)}, bf16[4,96,128]{2,1,0:T(8,128)(2,1)S(1)}, u32[]{:S(2)}, u32[]{:S(2)}) collective-permute-start(bf16[4,96,128]{2,1,0:T(8,128)(2,1)S(1)} %get-tuple-element.208), channel_id=1, source_target_pairs={{0,8},{1,9},{2,10},{3,11},{4,12},{5,13},{6,14},{7,15},{8,16},{9,17... | collective-permute-start | bytes 294920 | tf_op jit(solution)/shard_map/ppermute | solution.py:579
  166.5 7.8 %collective-permute-start.57 = (bf16[4,96,128]{2,1,0:T(8,128)(2,1)S(1)}, bf16[4,96,128]{2,1,0:T(8,128)(2,1)S(1)}, u32[]{:S(2)}, u32[]{:S(2)}) collective-permute-start(bf16[4,96,128]{2,1,0:T(8,128)(2,1)S(1)} %get-tuple-element.208), channel_id=1, source_target_pairs={{0,16},{1,17},{2,18},{3,19},{4,20},{5,21},{6,22},{7,23},{8,24},{9,... | collective-permute-start | bytes 294920 | tf_op jit(solution)/shard_map/ppermute | solution.py:579
  169.4 8.4 %collective-permute-start.50 = (bf16[4,96,128]{2,1,0:T(8,128)(2,1)S(1)}, bf16[4,96,128]{2,1,0:T(8,128)(2,1)S(1)}, u32[]{:S(2)}, u32[]{:S(2)}) collective-permute-start(bf16[4,96,128]{2,1,0:T(8,128)(2,1)S(1)} %get-tuple-element.209), channel_id=1, source_target_pairs={{0,2},{1,3},{2,0},{3,1},{4,6},{5,7},{6,4},{7,5},{8,10},{9,11},{10,... | collective-permute-start | bytes 294920 | tf_op jit(solution)/shard_map/ppermute | solution.py:583
  170.3 7.5 %collective-permute-start.51 = (bf16[4,96,128]{2,1,0:T(8,128)(2,1)S(1)}, bf16[4,96,128]{2,1,0:T(8,128)(2,1)S(1)}, u32[]{:S(2)}, u32[]{:S(2)}) collective-permute-start(bf16[4,96,128]{2,1,0:T(8,128)(2,1)S(1)} %get-tuple-element.209), channel_id=1, source_target_pairs={{0,3},{1,0},{2,1},{3,2},{4,7},{5,4},{6,5},{7,6},{8,11},{9,8},{10,9... | collective-permute-start | bytes 294920 | tf_op jit(solution)/shard_map/ppermute | solution.py:583
  173.3 6.8 %collective-permute-start.49 = (bf16[4,96,128]{2,1,0:T(8,128)(2,1)S(1)}, bf16[4,96,128]{2,1,0:T(8,128)(2,1)S(1)}, u32[]{:S(2)}, u32[]{:S(2)}) collective-permute-start(bf16[4,96,128]{2,1,0:T(8,128)(2,1)S(1)} %get-tuple-element.209), channel_id=1, source_target_pairs={{0,1},{1,2},{2,3},{3,0},{4,5},{5,6},{6,7},{7,4},{8,9},{9,10},{10,1... | collective-permute-start | bytes 294920 | tf_op jit(solution)/shard_map/ppermute | solution.py:583
  174.4 12.7 %collective-permute-start.59 = (bf16[4,4,96,128]{3,2,1,0:T(8,128)(2,1)S(1)}, bf16[4,4,96,128]{3,2,1,0:T(8,128)(2,1)S(1)}, u32[]{:S(2)}, u32[]{:S(2)}) collective-permute-start(bf16[4,4,96,128]{3,2,1,0:T(8,128)(2,1)S(1)} %pad_maximum_fusion.3.refs_3_), channel_id=1, source_target_pairs={{0,1},{1,2},{2,3},{3,0},{4,5},{5,6},{6,7},{7,4},{8,9},{9,10},{10,1... | collective-permute-start | bytes 1179656 | tf_op jit(solution)/shard_map/ppermute | solution.py:583
  175.7 11.5 %collective-permute-start.61 = (bf16[4,4,96,128]{3,2,1,0:T(8,128)(2,1)S(1)}, bf16[4,4,96,128]{3,2,1,0:T(8,128)(2,1)S(1)}, u32[]{:S(2)}, u32[]{:S(2)}) collective-permute-start(bf16[4,4,96,128]{3,2,1,0:T(8,128)(2,1)S(1)} %pad_maximum_fusion.3.refs_3_), channel_id=1, source_target_pairs={{0,3},{1,0},{2,1},{3,2},{4,7},{5,4},{6,5},{7,6},{8,11},{9,8},{10,9... | collective-permute-start | bytes 1179656 | tf_op jit(solution)/shard_map/ppermute | solution.py:583
  180.1 10.4 %collective-permute-start.52 = (bf16[4,4,96,128]{3,2,1,0:T(8,128)(2,1)S(1)}, bf16[4,4,96,128]{3,2,1,0:T(8,128)(2,1)S(1)}, u32[]{:S(2)}, u32[]{:S(2)}) collective-permute-start(bf16[4,4,96,128]{3,2,1,0:T(8,128)(2,1)S(1)} %pad_maximum_fusion.2.refs_0_), channel_id=1, source_target_pairs={{0,8},{1,9},{2,10},{3,11},{4,12},{5,13},{6,14},{7,15},{8,16},{9,17... | collective-permute-start | bytes 1179656 | tf_op jit(solution)/shard_map/ppermute | solution.py:579
  182.4 9.9 %collective-permute-start.54 = (bf16[4,4,96,128]{3,2,1,0:T(8,128)(2,1)S(1)}, bf16[4,4,96,128]{3,2,1,0:T(8,128)(2,1)S(1)}, u32[]{:S(2)}, u32[]{:S(2)}) collective-permute-start(bf16[4,4,96,128]{3,2,1,0:T(8,128)(2,1)S(1)} %pad_maximum_fusion.2.refs_0_), channel_id=1, source_target_pairs={{0,24},{1,25},{2,26},{3,27},{4,28},{5,29},{6,30},{7,31},{8,0},{9,1... | collective-permute-start | bytes 1179656 | tf_op jit(solution)/shard_map/ppermute | solution.py:579
  187.1 9.2 %collective-permute-start.60 = (bf16[2,4,96,128]{3,2,1,0:T(8,128)(2,1)S(1)}, bf16[2,4,96,128]{3,2,1,0:T(8,128)(2,1)S(1)}, u32[]{:S(2)}, u32[]{:S(2)}) collective-permute-start(bf16[2,4,96,128]{3,2,1,0:T(8,128)(2,1)S(1)} %slice.36), channel_id=1, source_target_pairs={{0,1},{1,2},{2,3},{3,0},{4,5},{5,6},{6,7},{7,4},{8,9},{9,10},{10,1... | collective-permute-start | bytes 589832 | tf_op jit(solution)/shard_map/ppermute | solution.py:583
  187.3 9.1 %collective-permute-start.62 = (bf16[2,4,96,128]{3,2,1,0:T(8,128)(2,1)S(1)}, bf16[2,4,96,128]{3,2,1,0:T(8,128)(2,1)S(1)}, u32[]{:S(2)}, u32[]{:S(2)}) collective-permute-start(bf16[2,4,96,128]{3,2,1,0:T(8,128)(2,1)S(1)} %slice.37), channel_id=1, source_target_pairs={{0,3},{1,0},{2,1},{3,2},{4,7},{5,4},{6,5},{7,6},{8,11},{9,8},{10,9... | collective-permute-start | bytes 589832 | tf_op jit(solution)/shard_map/ppermute | solution.py:583
  190.6 7.0 %collective-permute-start.53 = (bf16[2,4,96,128]{3,2,1,0:T(8,128)(2,1)S(1)}, bf16[2,4,96,128]{3,2,1,0:T(8,128)(2,1)S(1)}, u32[]{:S(2)}, u32[]{:S(2)}) collective-permute-start(bf16[2,4,96,128]{3,2,1,0:T(8,128)(2,1)S(1)} %slice.33), channel_id=1, source_target_pairs={{0,8},{1,9},{2,10},{3,11},{4,12},{5,13},{6,14},{7,15},{8,16},{9,17... | collective-permute-start | bytes 589832 | tf_op jit(solution)/shard_map/ppermute | solution.py:579
  192.3 5.7 %collective-permute-start.55 = (bf16[2,4,96,128]{3,2,1,0:T(8,128)(2,1)S(1)}, bf16[2,4,96,128]{3,2,1,0:T(8,128)(2,1)S(1)}, u32[]{:S(2)}, u32[]{:S(2)}) collective-permute-start(bf16[2,4,96,128]{3,2,1,0:T(8,128)(2,1)S(1)} %slice.34), channel_id=1, source_target_pairs={{0,24},{1,25},{2,26},{3,27},{4,28},{5,29},{6,30},{7,31},{8,0},{9,1... | collective-permute-start | bytes 589832 | tf_op jit(solution)/shard_map/ppermute | solution.py:579
  (15 other events, 59.5 us)
where the time goes:
time: 202 us; the launch traced here: 200 us
  starting transfers between devices  83.4 us (41%)
  waiting for transfers between devices  78.7 us (39%)
  Pallas kernels  35.4 us (18%)
    pallas_call x17, Pallas kernels, call(): pl.pallas_call(functools.partial(placed, body) if ins[0][1] is SMEM else...  35.4 us
    ppermute x29, starting transfers between devices, swap(): return lax.ppermute(value, 'section', [(s, s ^ k) for s in sources])  33.3 us
    ppermute x29, waiting for transfers between devices, swap(): return lax.ppermute(value, 'section', [(s, s ^ k) for s in sources])  32.4 us
    ppermute x14, starting transfers between devices, along_y(): lax.ppermute(value, 'rep', [(rep_of(x, z, y), rep_of(x, z, (y + k) % 4))...  22.3 us
    ppermute x14, starting transfers between devices, along_x(): lax.ppermute(value, 'rep', [(rep_of(x, z, y), rep_of((x + k) % 4, z, y))...  20.5 us
    ppermute x14, waiting for transfers between devices, along_x(): lax.ppermute(value, 'rep', [(rep_of(x, z, y), rep_of((x + k) % 4, z, y))...  13 us
    ppermute x14, waiting for transfers between devices, along_y(): lax.ppermute(value, 'rep', [(rep_of(x, z, y), rep_of(x, z, (y + k) % 4))...  11.8 us
    ppermute x1, waiting for transfers between devices, beside(): return lax.ppermute(value, ('section', 'rep'), pairs)  10.1 us
  transfers between devices with their start and end apart: 63, of which 35 were waited for; matrix products, arithmetic and copies ran while one was open for 0% of the time, Pallas kernels for 3%

commit v1 on v0

--- a/solution.py
+++ b/solution.py
@@ -524,12 +524,10 @@
             b[d][i] = gouts[s][to, :]
 
 
-def relay_body(a1, a3, a_lo, a_hi, b1, b3, b_lo, b_hi, a1_out, a3_out, b1_out, b3_out):
+def relay_body(a1, a3, a_lo, a_hi, a1_out, a3_out):
     for src, extra, at, dst in (
         (a1, a_lo, 0, a1_out),
         (a3, a_hi, 2, a3_out),
-        (b1, b_lo, 0, b1_out),
-        (b3, b_hi, 2, b3_out),
     ):
         for s in range(4):
             if at <= s < at + 2:
@@ -545,17 +543,23 @@
     return total.astype(BF)
 
 
-def second_body(sc, a0, a1, a2, b0, b1, b2, c0, c1, c2, c3, d0, d1, d2, d3, a_v, b_v):
-    x, y = sc[3], sc[5]
+def second_in_body(sc, a0, a1, a2, c0, c1, c2, c3, a_v):
     for s in range(4):
         a_v[s] = total_of([r[s] for r in (a0, a1, a2)])
-        b_v[s] = total_of([r[s] for r in (b0, b1, b2)])
-    rows, cols = c0.shape[1], d0.shape[2]
-    for k, (c, d) in enumerate(((c0, d0), (c1, d1), (c2, d2), (c3, d3))):
-        at = pl.ds(pl.multiple_of(((y + k) % 4) * rows, rows), rows)
-        to = pl.ds(pl.multiple_of(((x + k) % 4) * cols, cols), cols)
+    rows = c0.shape[1]
+    for k, c in enumerate((c0, c1, c2, c3)):
+        at = pl.ds(pl.multiple_of(((sc[5] + k) % 4) * rows, rows), rows)
         for s in range(4):
             c[s] = a_v[s, at, :]
+
+
+def second_out_body(sc, b0, b1, b2, d0, d1, d2, d3, b_v):
+    for s in range(4):
+        b_v[s] = total_of([r[s] for r in (b0, b1, b2)])
+    cols = d0.shape[2]
+    for k, d in enumerate((d0, d1, d2, d3)):
+        to = pl.ds(pl.multiple_of(((sc[3] + k) % 4) * cols, cols), cols)
+        for s in range(4):
             d[s] = b_v[s, :, to]
 
 
@@ -801,22 +805,25 @@
     )
     a, b = cut[:5], cut[5:]
     far_a, far_b = (along_x(a[2], 1), along_x(a[3], 3)), (along_y(b[2], 1), along_y(b[3], 3))
-    to_a, back_a, to_b, back_b = call(
-        relay_body,
-        [((4, rows, rank), BF, VMEM)] * 2 + [((4, low, quarter), BF, VMEM)] * 2,
-        [],
-        [(v, VMEM) for v in (a[1], a[4], *far_a, b[1], b[4], *far_b)],
-    )
+    whole_a, whole_b = (4, rows, rank), (4, low, quarter)
+    to_a, back_a = call(relay_body, [(whole_a, BF, VMEM)] * 2, [], [(v, VMEM) for v in (a[1], a[4], *far_a)])
+    to_b, back_b = call(relay_body, [(whole_b, BF, VMEM)] * 2, [], [(v, VMEM) for v in (b[1], b[4], *far_b)])
     a = [a[0], along_x(to_a, 1), along_x(back_a, 3)]
     b = [b[0], along_y(to_b, 1), along_y(back_b, 3)]
-    cut = call(
-        second_body,
-        [((4, rows // 4, rank), BF, VMEM)] * 4 + [((4, low, rows), BF, VMEM)] * 4,
-        [pltpu.VMEM((4, rows, rank), BF), pltpu.VMEM((4, low, quarter), BF)],
-        [(sc, SMEM)] + [(v, VMEM) for v in a + b],
-    )
-    a = [cut[0]] + [along_y(cut[k], k) for k in (1, 2, 3)]
-    b = [cut[4]] + [along_x(cut[4 + k], k) for k in (1, 2, 3)]
+    cut_a = call(
+        second_in_body,
+        [((4, rows // 4, rank), BF, VMEM)] * 4,
+        [pltpu.VMEM(whole_a, BF)],
+        [(sc, SMEM)] + [(v, VMEM) for v in a],
+    )
+    cut_b = call(
+        second_out_body,
+        [((4, low, rows), BF, VMEM)] * 4,
+        [pltpu.VMEM(whole_b, BF)],
+        [(sc, SMEM)] + [(v, VMEM) for v in b],
+    )
+    a = [cut_a[0]] + [along_y(cut_a[k], k) for k in (1, 2, 3)]
+    b = [cut_b[0]] + [along_x(cut_b[k], k) for k in (1, 2, 3)]
     (both,) = call(
         third_body,
         [((4, rows // 2, rank), BF, VMEM)],

time: 202 us -> 200 us (0.990)
  waiting for transfers between devices: 78.7 us -> 73.2 us
  starting transfers between devices: 83.4 us -> 85.6 us
    ppermute x14, waiting for transfers between devices: 13 us -> 2.62 us  [along_x(): lax.ppermute(value, 'rep', [(rep_of(x, z, y), rep_of((x + k) % 4, z, y))...]
    ppermute x14, waiting for transfers between devices: 11.8 us -> 16.6 us  [along_y(): lax.ppermute(value, 'rep', [(rep_of(x, z, y), rep_of(x, z, (y + k) % 4))...]
    pallas_call x17 -> x19, Pallas kernels: 35.4 us -> 36.1 us  [call(): pl.pallas_call(functools.partial(placed, body) if ins[0][1] is SMEM else...]
  transfers between devices with their start and end apart: 63 -> 63, of which waited for: 35 -> 30; matrix products, arithmetic and copies ran while one was open for 0% -> 0% of each run, Pallas kernels for 3% -> 4%
where the time goes in v1:
time: 200 us; the launch traced here: 197 us
  starting transfers between devices  85.6 us (43%)
  waiting for transfers between devices  73.2 us (37%)
  Pallas kernels  36.1 us (18%)
    pallas_call x19, Pallas kernels, call(): pl.pallas_call(functools.partial(placed, body) if ins[0][1] is SMEM else...  36.1 us
    ppermute x29, starting transfers between devices, swap(): return lax.ppermute(value, 'section', [(s, s ^ k) for s in sources])  33.3 us
    ppermute x29, waiting for transfers between devices, swap(): return lax.ppermute(value, 'section', [(s, s ^ k) for s in sources])  32.4 us
    ppermute x14, starting transfers between devices, along_y(): lax.ppermute(value, 'rep', [(rep_of(x, z, y), rep_of(x, z, (y + k) % 4))...  22.7 us
    ppermute x14, starting transfers between devices, along_x(): lax.ppermute(value, 'rep', [(rep_of(x, z, y), rep_of((x + k) % 4, z, y))...  22.4 us
    ppermute x14, waiting for transfers between devices, along_y(): lax.ppermute(value, 'rep', [(rep_of(x, z, y), rep_of(x, z, (y + k) % 4))...  16.6 us
    ppermute x1, waiting for transfers between devices, beside(): return lax.ppermute(value, ('section', 'rep'), pairs)  10.1 us
    ppermute x4, waiting for transfers between devices, beside_along(): return lax.ppermute(value, ('section', 'rep'), pairs)  7.41 us
  transfers between devices with their start and end apart: 63, of which 30 were waited for; matrix products, arithmetic and copies ran while one was open for 0% of the time, Pallas kernels for 4%

profile of v1, /device:TPU:64, one launch (start us, length us, event | category | flops | bytes accessed | tf_op | source)
XLA Modules:
  0.0 197.2 jit_solution(9593874387038627379)
XLA Ops:
  1.4 2.5 %shard_map.95 = (bf16[256,1536]{1,0:T(8,128)(2,1)S(1)}, bf16[256,1536]{1,0:T(8,128)(2,1)S(1)}, bf16[1536,128]{1,0:T(8,128)(2,1)S(1)}, bf16[128,1536]{1,0:T(8,128)(2,1)S(1)}, bf16[1536,128]{1,0:T(8,128)(2,1)S(1)}) custom-call(s32[2,1]{1,0:T(2,128)S(1)} %copy.25.ids, bf16[1,2,2,128,6144]{4,3,2,1,0:T(8,128)(2,1)} %refs_6_.5, bf16[1,1,6144,128]{3,2,1,0:T(8,128)(2,1)} %refs_8_.5, ...), custom_call_target="tpu_custom_call" | custom-call | flops 100000000 | bytes 4000000 | tf_op jit(solution)/shard_map/pallas_call | solution.py:49
  4.7 10.1 %collective-permute-done = bf16[1536,128]{1,0:T(8,128)(2,1)S(1)} collective-permute-done((bf16[1536,128]{1,0:T(8,128)(2,1)S(1)}, bf16[1536,128]{1,0:T(8,128)(2,1)S(1)}, u32[]{:S(2)}, u32[]{:S(2)}) %collective-permute-start) | collective-permute-done | bytes 393248 | tf_op jit(solution)/shard_map/ppermute | solution.py:656
  16.4 1.9 collective-permute-start.8
  18.4 1.7 collective-permute-start.3
  20.7 4.2 %collective-permute-done.3 = bf16[768,128]{1,0:T(8,128)(2,1)S(1)} collective-permute-done((bf16[768,128]{1,0:T(8,128)(2,1)S(1)}, bf16[768,128]{1,0:T(8,128)(2,1)S(1)}, u32[]{:S(2)}, u32[]{:S(2)}) %collective-permute-start.3) | collective-permute-done | bytes 196640 | tf_op jit(solution)/shard_map/ppermute | solution.py:660
  31.8 4.2 %collective-permute-done.8.refs_7_ = bf16[256,1536]{1,0:T(8,128)(2,1)S(1)} collective-permute-done((bf16[256,1536]{1,0:T(8,128)(2,1)S(1)}, bf16[256,1536]{1,0:T(8,128)(2,1)S(1)}, u32[]{:S(2)}, u32[]{:S(2)}) %collective-permute-start.8) | collective-permute-done | bytes 786464 | tf_op jit(solution)/shard_map/ppermute | solution.py:649
  38.6 4.7 %shard_map.97 = (f32[256,1536]{1,0:T(8,128)S(1)}, bf16[256,1536]{1,0:T(8,128)(2,1)S(1)}, bf16[272,128]{1,0:T(8,128)(2,1)S(1)}, f32[256,128]{1,0:T(8,128)S(1)}, f...) custom-call(s32[2,1]{1,0:T(2,128)S(1)} %copy.25.ids, ...), custom_call_target="tpu_custom_call" | custom-call | flops 100000000 | bytes 4000000 | tf_op jit(solution)/shard_map/pallas_call | solution.py:49
  43.3 2.8 %collective-permute-start.15 = (bf16[256,1536]{1,0:T(8,128)(2,1)S(1)}, bf16[256,1536]{1,0:T(8,128)(2,1)S(1)}, u32[]{:S(2)}, u32[]{:S(2)}) collective-permute-start(bf16[256,1536]{1,0:T(8,128)(2,1)S(1)} %get-tuple-element.134), channel_id=1, source_target_pairs={{32,0},{64,96},{33,1},{65,97},{34,2},{66,98},{35,3},{67,99},{36,4}... | collective-permute-start | bytes 2359304 | tf_op jit(solution)/shard_map/ppermute | solution.py:649
  46.3 2.5 %collective-permute-start.13 = (bf16[272,128]{1,0:T(8,128)(2,1)S(1)}, bf16[272,128]{1,0:T(8,128)(2,1)S(1)}, u32[]{:S(2)}, u32[]{:S(2)}) collective-permute-start(bf16[272,128]{1,0:T(8,128)(2,1)S(1)} %get-tuple-element.132.refs_0_), channel_id=1, source_target_pairs={{0,64},{32,96},{64,0},{96,32},{1,65},{33,97},{65,1},{97,33},{2,66}... | collective-permute-start | bytes 208904 | tf_op jit(solution)/shard_map/ppermute | solution.py:649
  49.6 2.7 %collective-permute-done.13.refs_2_ = bf16[272,128]{1,0:T(8,128)(2,1)S(1)} collective-permute-done((bf16[272,128]{1,0:T(8,128)(2,1)S(1)}, bf16[272,128]{1,0:T(8,128)(2,1)S(1)}, u32[]{:S(2)}, u32[]{:S(2)}) %collective-permute-start.13) | collective-permute-done | bytes 69664 | tf_op jit(solution)/shard_map/ppermute | solution.py:649
  52.4 2.4 %collective-permute-done.14.refs_3_ = bf16[272,128]{1,0:T(8,128)(2,1)S(1)} collective-permute-done((bf16[272,128]{1,0:T(8,128)(2,1)S(1)}, bf16[272,128]{1,0:T(8,128)(2,1)S(1)}, u32[]{:S(2)}, u32[]{:S(2)}) %collective-permute-start.14) | collective-permute-done | bytes 69664 | tf_op jit(solution)/shard_map/ppermute | solution.py:649
  54.7 3.8 %shard_map.98 = (f32[256,1536]{1,0:T(8,128)S(1)}, bf16[256,1536]{1,0:T(8,128)(2,1)S(1)}, bf16[272,128]{1,0:T(8,128)(2,1)S(1)}, f32[256,128]{1,0:T(8,128)S(1)}, f...) custom-call(s32[2,1]{1,0:T(2,128)S(1)} %copy.25.ids, ...), custom_call_target="tpu_custom_call" | custom-call | flops 100000000 | bytes 4000000 | tf_op jit(solution)/shard_map/pallas_call | solution.py:49
  62.1 2.9 %collective-permute-done.17.refs_2_ = bf16[272,128]{1,0:T(8,128)(2,1)S(1)} collective-permute-done((bf16[272,128]{1,0:T(8,128)(2,1)S(1)}, bf16[272,128]{1,0:T(8,128)(2,1)S(1)}, u32[]{:S(2)}, u32[]{:S(2)}) %collective-permute-start.17) | collective-permute-done | bytes 69664 | tf_op jit(solution)/shard_map/ppermute | solution.py:649
  66.3 4.2 %shard_map.99 = (f32[256,1536]{1,0:T(8,128)S(1)}, bf16[256,1536]{1,0:T(8,128)(2,1)S(1)}, bf16[272,128]{1,0:T(8,128)(2,1)S(1)}, f32[256,128]{1,0:T(8,128)S(1)}, f...) custom-call(s32[2,1]{1,0:T(2,128)S(1)} %copy.25.ids, ...), custom_call_target="tpu_custom_call" | custom-call | flops 100000000 | bytes 4000000 | tf_op jit(solution)/shard_map/pallas_call | solution.py:49
  70.6 3.1 %collective-permute-start.20 = (bf16[272,128]{1,0:T(8,128)(2,1)S(1)}, bf16[272,128]{1,0:T(8,128)(2,1)S(1)}, u32[]{:S(2)}, u32[]{:S(2)}) collective-permute-start(bf16[272,128]{1,0:T(8,128)(2,1)S(1)} %get-tuple-element.137.refs_4_), channel_id=1, source_target_pairs={{0,64},{32,96},{64,0},{96,32},{1,65},{33,97},{65,1},{97,33},{2,66}... | collective-permute-start | bytes 208904 | tf_op jit(solution)/shard_map/ppermute | solution.py:649
  74.0 2.7 %collective-permute-done.20.refs_6_ = bf16[272,128]{1,0:T(8,128)(2,1)S(1)} collective-permute-done((bf16[272,128]{1,0:T(8,128)(2,1)S(1)}, bf16[272,128]{1,0:T(8,128)(2,1)S(1)}, u32[]{:S(2)}, u32[]{:S(2)}) %collective-permute-start.20) | collective-permute-done | bytes 69664 | tf_op jit(solution)/shard_map/ppermute | solution.py:649
  76.7 2.6 %collective-permute-done.21.refs_7_ = bf16[272,128]{1,0:T(8,128)(2,1)S(1)} collective-permute-done((bf16[272,128]{1,0:T(8,128)(2,1)S(1)}, bf16[272,128]{1,0:T(8,128)(2,1)S(1)}, u32[]{:S(2)}, u32[]{:S(2)}) %collective-permute-start.21) | collective-permute-done | bytes 69664 | tf_op jit(solution)/shard_map/ppermute | solution.py:649
  79.3 3.7 %shard_map.100 = (bf16[256,1536]{1,0:T(8,128)(2,1)S(1)}, bf16[256,128]{1,0:T(8,128)(2,1)S(1)}, bf16[256,128]{1,0:T(8,128)(2,1)S(1)}, bf16[256,1536]{1,0:T(8,128)(2,1)S(1)}, f32[256,128]{1,0:T(8,128)S(1)}) custom-call(s32[2,1]{1,0:T(2,128)S(1)} %copy.25.ids, bf16[272,128]{1,0:T(8,128)(2,1)S(1)} %shard_map.96.refs_0_, ...), custom_call_target="tpu_custom_call" | custom-call | flops 100000000 | bytes 4000000 | tf_op jit(solution)/shard_map/pallas_call | solution.py:49
  84.8 1.7 collective-permute-start.24
  86.4 2.6 %collective-permute-done.23.refs_2_ = bf16[256,128]{1,0:T(8,128)(2,1)S(1)} collective-permute-done((bf16[256,128]{1,0:T(8,128)(2,1)S(1)}, bf16[256,128]{1,0:T(8,128)(2,1)S(1)}, u32[]{:S(2)}, u32[]{:S(2)}) %collective-permute-start.23) | collective-permute-done | bytes 65568 | tf_op jit(solution)/shard_map/ppermute | solution.py:649
  90.5 3.2 %shard_map.101 = (bf16[256,1536]{1,0:T(8,128)(2,1)S(1)}, bf16[256,128]{1,0:T(8,128)(2,1)S(1)}, bf16[256,128]{1,0:T(8,128)(2,1)S(1)}) custom-call(s32[2,1]{1,0:T(2,128)S(1)} %copy.25.ids, bf16[256,128]{1,0:T(8,128)(2,1)S(1)} %get-tuple-element.141.refs_0_, bf16[256,128]{1,0:T(8,128)(2,1)S(1)} %collective-permute-done.22.refs_1_, ...), custom_call_target="tpu_custom_call" | custom-call | flops 100000000 | bytes 4000000 | tf_op jit(solution)/shard_map/pallas_call | solution.py:49
  94.0 1.9 collective-permute-start.26
  97.2 2.1 %shard_map.103 = (bf16[1536,128]{1,0:T(8,128)(2,1)S(1)}, bf16[128,1536]{1,0:T(8,128)(2,1)S(1)}) custom-call(s32[2,1]{1,0:T(2,128)S(1)} %copy.25.ids, bf16[256,1536]{1,0:T(8,128)(2,1)S(1)} %get-tuple-element.152.refs_0_, f32[256,128]{1,0:T(8,128)S(1)} %get-tuple-element.153.refs_1_, bf16[2,128,6144]{2,1,0:T(8,128)(2,1)} %refs_2_.5, ...), custom_call_target="tpu_custom_call" | custom-call | flops 100000000 | bytes 4000000 | tf_op jit(solution)/shard_map/pallas_call | solution.py:49
  101.4 3.2 %shard_map.104 = (bf16[256,1536]{1,0:T(8,128)(2,1)S(1)}, bf16[256,128]{1,0:T(8,128)(2,1)S(1)}, bf16[256,128]{1,0:T(8,128)(2,1)S(1)}) custom-call(s32[2,1]{1,0:T(2,128)S(1)} %copy.25.ids, bf16[256,128]{1,0:T(8,128)(2,1)S(1)} %get-tuple-element.158.refs_0_, bf16[256,128]{1,0:T(8,128)(2,1)S(1)} %collective-permute-done.25.refs_1_, ...), custom_call_target="tpu_custom_call" | custom-call | flops 100000000 | bytes 4000000 | tf_op jit(solution)/shard_map/pallas_call | solution.py:49
  104.9 1.7 collective-permute-start.29
  108.6 2.1 %collective-permute-done.29.refs_2_ = bf16[256,128]{1,0:T(8,128)(2,1)S(1)} collective-permute-done((bf16[256,128]{1,0:T(8,128)(2,1)S(1)}, bf16[256,128]{1,0:T(8,128)(2,1)S(1)}, u32[]{:S(2)}, u32[]{:S(2)}) %collective-permute-start.29) | collective-permute-done | bytes 65568 | tf_op jit(solution)/shard_map/ppermute | solution.py:649
  114.2 2.5 %collective-permute-start.39 = (bf16[2,32,1536]{2,1,0:T(8,128)(2,1)S(1)}, bf16[2,32,1536]{2,1,0:T(8,128)(2,1)S(1)}, u32[]{:S(2)}, u32[]{:S(2)}) collective-permute-start(bf16[2,32,1536]{2,1,0:T(8,128)(2,1)S(1)} %get-tuple-element.195), channel_id=1, source_target_pairs={{0,3},{1,0},{2,1},{3,2},{4,7},{5,4},{6,5},{7,6},{8,11},{9,8},{10,9... | collective-permute-start | bytes 589832 | tf_op jit(solution)/shard_map/ppermute | solution.py:587
  118.2 1.8 collective-permute-start.32
  120.0 1.7 collective-permute-done.38.a_lo
  123.2 1.9 collective-permute-start.41
  126.7 1.7 collective-permute-start.34
  128.5 4.8 %collective-permute-done.40.refs_1_ = bf16[4,32,1536]{2,1,0:T(8,128)(2,1)S(1)} collective-permute-done((bf16[4,32,1536]{2,1,0:T(8,128)(2,1)S(1)}, bf16[4,32,1536]{2,1,0:T(8,128)(2,1)S(1)}, u32[]{:S(2)}, u32[]{:S(2)}) %collective-permute-start.40) | collective-permute-done | bytes 393248 | tf_op jit(solution)/shard_map/ppermute | solution.py:587
  135.7 2.7 %collective-permute-start.43 = (bf16[4,32,384]{2,1,0:T(8,128)(2,1)S(1)}, bf16[4,32,384]{2,1,0:T(8,128)(2,1)S(1)}, u32[]{:S(2)}, u32[]{:S(2)}) collective-permute-start(bf16[4,32,384]{2,1,0:T(8,128)(2,1)S(1)} %get-tuple-element.200), channel_id=1, source_target_pairs={{0,16},{1,17},{2,18},{3,19},{4,20},{5,21},{6,22},{7,23},{8,24},{9,... | collective-permute-start | bytes 294920 | tf_op jit(solution)/shard_map/ppermute | solution.py:583
  141.5 3.6 %collective-permute-start.36 = (bf16[4,96,128]{2,1,0:T(8,128)(2,1)S(1)}, bf16[4,96,128]{2,1,0:T(8,128)(2,1)S(1)}, u32[]{:S(2)}, u32[]{:S(2)}) collective-permute-start(bf16[4,96,128]{2,1,0:T(8,128)(2,1)S(1)} %get-tuple-element.189), channel_id=1, source_target_pairs={{0,2},{1,3},{2,0},{3,1},{4,6},{5,7},{6,4},{7,5},{8,10},{9,11},{10,... | collective-permute-start | bytes 294920 | tf_op jit(solution)/shard_map/ppermute | solution.py:587
  146.5 2.2 %collective-permute-done.36.a2 = bf16[4,96,128]{2,1,0:T(8,128)(2,1)S(1)} collective-permute-done((bf16[4,96,128]{2,1,0:T(8,128)(2,1)S(1)}, bf16[4,96,128]{2,1,0:T(8,128)(2,1)S(1)}, u32[]{:S(2)}, u32[]{:S(2)}) %collective-permute-start.36) | collective-permute-done | bytes 98336 | tf_op jit(solution)/shard_map/ppermute | solution.py:587
  149.8 1.6 collective-permute-start.45
  151.5 4.1 %collective-permute-done.45 = bf16[4,192,128]{2,1,0:T(8,128)(2,1)S(1)} collective-permute-done((bf16[4,192,128]{2,1,0:T(8,128)(2,1)S(1)}, bf16[4,192,128]{2,1,0:T(8,128)(2,1)S(1)}, u32[]{:S(2)}, u32[]{:S(2)}) %collective-permute-start.45) | collective-permute-done | bytes 196640 | tf_op jit(solution)/shard_map/ppermute | solution.py:591
  155.8 1.9 collective-permute-start.47
  159.1 2.3 %collective-permute-done.47 = bf16[192,128]{1,0:T(8,128)(2,1)S(1)} collective-permute-done((bf16[192,128]{1,0:T(8,128)(2,1)S(1)}, bf16[192,128]{1,0:T(8,128)(2,1)S(1)}, u32[]{:S(2)}, u32[]{:S(2)}) %collective-permute-start.47) | collective-permute-done | bytes 49184 | tf_op jit(solution)/shard_map/ppermute | solution.py:649
  164.5 1.9 collective-permute-start.58
  167.9 1.9 collective-permute-start.51
  172.8 2.5 %collective-permute-start.61 = (bf16[4,4,96,128]{3,2,1,0:T(8,128)(2,1)S(1)}, bf16[4,4,96,128]{3,2,1,0:T(8,128)(2,1)S(1)}, u32[]{:S(2)}, u32[]{:S(2)}) collective-permute-start(bf16[4,4,96,128]{3,2,1,0:T(8,128)(2,1)S(1)} %pad_maximum_fusion.3.refs_3_), channel_id=1, source_target_pairs={{0,3},{1,0},{2,1},{3,2},{4,7},{5,4},{6,5},{7,6},{8,11},{9,8},{10,9... | collective-permute-start | bytes 1179656 | tf_op jit(solution)/shard_map/ppermute | solution.py:587
  175.3 2.9 %collective-permute-done.49 = bf16[4,96,128]{2,1,0:T(8,128)(2,1)S(1)} collective-permute-done((bf16[4,96,128]{2,1,0:T(8,128)(2,1)S(1)}, bf16[4,96,128]{2,1,0:T(8,128)(2,1)S(1)}, u32[]{:S(2)}, u32[]{:S(2)}) %collective-permute-start.49) | collective-permute-done | bytes 98336 | tf_op jit(solution)/shard_map/ppermute | solution.py:587
  178.3 3.2 %collective-permute-start.54 = (bf16[4,4,96,128]{3,2,1,0:T(8,128)(2,1)S(1)}, bf16[4,4,96,128]{3,2,1,0:T(8,128)(2,1)S(1)}, u32[]{:S(2)}, u32[]{:S(2)}) collective-permute-start(bf16[4,4,96,128]{3,2,1,0:T(8,128)(2,1)S(1)} %pad_maximum_fusion.2.refs_0_), channel_id=1, source_target_pairs={{0,24},{1,25},{2,26},{3,27},{4,28},{5,29},{6,30},{7,31},{8,0},{9,1... | collective-permute-start | bytes 1179656 | tf_op jit(solution)/shard_map/ppermute | solution.py:583
  181.5 3.5 %collective-permute-done.59.refs_4_ = bf16[4,4,96,128]{3,2,1,0:T(8,128)(2,1)S(1)} collective-permute-done((bf16[4,4,96,128]{3,2,1,0:T(8,128)(2,1)S(1)}, bf16[4,4,96,128]{3,2,1,0:T(8,128)(2,1)S(1)}, u32[]{:S(2)}, u32[]{:S(2)}) %collective-permute-start.59) | collective-permute-done | bytes 393248 | tf_op jit(solution)/shard_map/ppermute | solution.py:587
  185.1 3.3 %collective-permute-start.62 = (bf16[2,4,96,128]{3,2,1,0:T(8,128)(2,1)S(1)}, bf16[2,4,96,128]{3,2,1,0:T(8,128)(2,1)S(1)}, u32[]{:S(2)}, u32[]{:S(2)}) collective-permute-start(bf16[2,4,96,128]{3,2,1,0:T(8,128)(2,1)S(1)} %slice.37), channel_id=1, source_target_pairs={{0,3},{1,0},{2,1},{3,2},{4,7},{5,4},{6,5},{7,6},{8,11},{9,8},{10,9... | collective-permute-start | bytes 589832 | tf_op jit(solution)/shard_map/ppermute | solution.py:587
  188.5 3.3 %collective-permute-start.55 = (bf16[2,4,96,128]{3,2,1,0:T(8,128)(2,1)S(1)}, bf16[2,4,96,128]{3,2,1,0:T(8,128)(2,1)S(1)}, u32[]{:S(2)}, u32[]{:S(2)}) collective-permute-start(bf16[2,4,96,128]{3,2,1,0:T(8,128)(2,1)S(1)} %slice.34), channel_id=1, source_target_pairs={{0,24},{1,25},{2,26},{3,27},{4,28},{5,29},{6,30},{7,31},{8,0},{9,1... | collective-permute-start | bytes 589832 | tf_op jit(solution)/shard_map/ppermute | solution.py:583
  191.8 2.4 %shard_map.112 = (bf16[1,1,6144,128]{3,2,1,0:T(8,128)(2,1)}, bf16[1,1,128,6144]{3,2,1,0:T(8,128)(2,1)}) custom-call(s32[2,1]{1,0:T(2,128)S(1)} %copy.25.ids, bf16[4,4,96,128]{3,2,1,0:T(8,128)(2,1)S(1)} %pad_maximum_fusion.2.refs_0_, bf16[4,4,96,128]{3,2,1,0:T(8,128)(2,1)S(1)} %collective-permute-done.52.refs_1_, ...), custom_call_target="tpu_custom_call" | custom-call | flops 100000000 | bytes 4000000 | tf_op jit(solution)/shard_map/pallas_call | solution.py:49
  (111 shorter events, 57.2 us)
Async XLA Ops:
  3.9 10.9 %collective-permute-start = (bf16[1536,128]{1,0:T(8,128)(2,1)S(1)}, bf16[1536,128]{1,0:T(8,128)(2,1)S(1)}, u32[]{:S(2)}, u32[]{:S(2)}) collective-permute-start(bf16[1536,128]{1,0:T(8,128)(2,1)S(1)} %get-tuple-element.103), channel_id=1, source_target_pairs={{0,68},{1,69},{2,70},{3,71},{4,64},{5,65},{6,66},{7,67},{8,76},{9,... | collective-permute-start | bytes 1179656 | tf_op jit(solution)/shard_map/ppermute | solution.py:656
  14.8 5.8 %collective-permute-start.1 = (bf16[768,128]{1,0:T(8,128)(2,1)S(1)}, bf16[768,128]{1,0:T(8,128)(2,1)S(1)}, u32[]{:S(2)}, u32[]{:S(2)}) collective-permute-start(bf16[768,128]{1,0:T(8,128)(2,1)S(1)} %get-tuple-element.205), channel_id=1, source_target_pairs={{0,8},{1,9},{2,10},{3,11},{4,12},{5,13},{6,14},{7,15},{8,0},{9,1},... | collective-permute-start | bytes 589832 | tf_op jit(solution)/shard_map/ppermute | solution.py:660
  16.4 19.6 %collective-permute-start.8 = (bf16[256,1536]{1,0:T(8,128)(2,1)S(1)}, bf16[256,1536]{1,0:T(8,128)(2,1)S(1)}, u32[]{:S(2)}, u32[]{:S(2)}) collective-permute-start(bf16[256,1536]{1,0:T(8,128)(2,1)S(1)} %get-tuple-element.117), channel_id=1, source_target_pairs={{0,64},{32,96},{64,0},{96,32},{1,65},{33,97},{65,1},{97,33},{2,66}... | collective-permute-start | bytes 2359304 | tf_op jit(solution)/shard_map/ppermute | solution.py:649
  18.4 6.6 %collective-permute-start.3 = (bf16[768,128]{1,0:T(8,128)(2,1)S(1)}, bf16[768,128]{1,0:T(8,128)(2,1)S(1)}, u32[]{:S(2)}, u32[]{:S(2)}) collective-permute-start(bf16[768,128]{1,0:T(8,128)(2,1)S(1)} %get-tuple-element.204), channel_id=1, source_target_pairs={{0,33},{1,32},{2,35},{3,34},{4,37},{5,36},{6,39},{7,38},{8,41},{9,... | collective-permute-start | bytes 589832 | tf_op jit(solution)/shard_map/ppermute | solution.py:660
  25.9 11.5 %collective-permute-start.6 = (bf16[1536,128]{1,0:T(8,128)(2,1)S(1)}, bf16[1536,128]{1,0:T(8,128)(2,1)S(1)}, u32[]{:S(2)}, u32[]{:S(2)}) collective-permute-start(bf16[1536,128]{1,0:T(8,128)(2,1)S(1)} %pad_maximum_fusion.refs_12_), channel_id=1, source_target_pairs={{0,1},{1,0},{2,3},{3,2},{4,5},{5,4},{6,7},{7,6},{8,9},{9,8},{10,11... | collective-permute-start | bytes 1179656 | tf_op jit(solution)/shard_map/ppermute | solution.py:660
  27.5 11.2 %collective-permute-start.7 = (bf16[1536,128]{1,0:T(8,128)(2,1)S(1)}, bf16[1536,128]{1,0:T(8,128)(2,1)S(1)}, u32[]{:S(2)}, u32[]{:S(2)}) collective-permute-start(bf16[1536,128]{1,0:T(8,128)(2,1)S(1)} %pad_maximum_fusion.1.refs_14_), channel_id=1, source_target_pairs={{0,8},{1,9},{2,10},{3,11},{4,12},{5,13},{6,14},{7,15},{8,0},{9,1},... | collective-permute-start | bytes 1179656 | tf_op jit(solution)/shard_map/ppermute | solution.py:660
  29.3 9.3 %collective-permute-start.10 = (bf16[272,128]{1,0:T(8,128)(2,1)S(1)}, bf16[272,128]{1,0:T(8,128)(2,1)S(1)}, u32[]{:S(2)}, u32[]{:S(2)}) collective-permute-start(bf16[272,128]{1,0:T(8,128)(2,1)S(1)} %shard_map.96.refs_0_), channel_id=1, source_target_pairs={{0,64},{96,32},{1,65},{97,33},{2,66},{98,34},{3,67},{99,35},{4,68}... | collective-permute-start | bytes 208904 | tf_op jit(solution)/shard_map/ppermute | solution.py:649
  31.1 7.5 %collective-permute-start.11 = (bf16[272,128]{1,0:T(8,128)(2,1)S(1)}, bf16[272,128]{1,0:T(8,128)(2,1)S(1)}, u32[]{:S(2)}, u32[]{:S(2)}) collective-permute-start(bf16[272,128]{1,0:T(8,128)(2,1)S(1)} %shard_map.96.refs_0_), channel_id=1, source_target_pairs={{0,96},{96,0},{1,97},{97,1},{2,98},{98,2},{3,99},{99,3},{4,100},{1... | collective-permute-start | bytes 208904 | tf_op jit(solution)/shard_map/ppermute | solution.py:649
  43.3 11.4 %collective-permute-start.15 = (bf16[256,1536]{1,0:T(8,128)(2,1)S(1)}, bf16[256,1536]{1,0:T(8,128)(2,1)S(1)}, u32[]{:S(2)}, u32[]{:S(2)}) collective-permute-start(bf16[256,1536]{1,0:T(8,128)(2,1)S(1)} %get-tuple-element.134), channel_id=1, source_target_pairs={{32,0},{64,96},{33,1},{65,97},{34,2},{66,98},{35,3},{67,99},{36,4}... | collective-permute-start | bytes 2359304 | tf_op jit(solution)/shard_map/ppermute | solution.py:649
  46.3 6.1 %collective-permute-start.13 = (bf16[272,128]{1,0:T(8,128)(2,1)S(1)}, bf16[272,128]{1,0:T(8,128)(2,1)S(1)}, u32[]{:S(2)}, u32[]{:S(2)}) collective-permute-start(bf16[272,128]{1,0:T(8,128)(2,1)S(1)} %get-tuple-element.132.refs_0_), channel_id=1, source_target_pairs={{0,64},{32,96},{64,0},{96,32},{1,65},{33,97},{65,1},{97,33},{2,66}... | collective-permute-start | bytes 208904 | tf_op jit(solution)/shard_map/ppermute | solution.py:649
  48.7 6.0 %collective-permute-start.14 = (bf16[272,128]{1,0:T(8,128)(2,1)S(1)}, bf16[272,128]{1,0:T(8,128)(2,1)S(1)}, u32[]{:S(2)}, u32[]{:S(2)}) collective-permute-start(bf16[272,128]{1,0:T(8,128)(2,1)S(1)} %get-tuple-element.132.refs_0_), channel_id=1, source_target_pairs={{0,96},{32,64},{64,32},{96,0},{1,97},{33,65},{65,33},{97,1},{2,98}... | collective-permute-start | bytes 208904 | tf_op jit(solution)/shard_map/ppermute | solution.py:649
  59.2 5.8 %collective-permute-start.17 = (bf16[272,128]{1,0:T(8,128)(2,1)S(1)}, bf16[272,128]{1,0:T(8,128)(2,1)S(1)}, u32[]{:S(2)}, u32[]{:S(2)}) collective-permute-start(bf16[272,128]{1,0:T(8,128)(2,1)S(1)} %get-tuple-element.135.refs_0_), channel_id=1, source_target_pairs={{0,64},{32,96},{64,0},{96,32},{1,65},{33,97},{65,1},{97,33},{2,66}... | collective-permute-start | bytes 208904 | tf_op jit(solution)/shard_map/ppermute | solution.py:649
  70.6 6.1 %collective-permute-start.20 = (bf16[272,128]{1,0:T(8,128)(2,1)S(1)}, bf16[272,128]{1,0:T(8,128)(2,1)S(1)}, u32[]{:S(2)}, u32[]{:S(2)}) collective-permute-start(bf16[272,128]{1,0:T(8,128)(2,1)S(1)} %get-tuple-element.137.refs_4_), channel_id=1, source_target_pairs={{0,64},{32,96},{64,0},{96,32},{1,65},{33,97},{65,1},{97,33},{2,66}... | collective-permute-start | bytes 208904 | tf_op jit(solution)/shard_map/ppermute | solution.py:649
  73.7 5.7 %collective-permute-start.21 = (bf16[272,128]{1,0:T(8,128)(2,1)S(1)}, bf16[272,128]{1,0:T(8,128)(2,1)S(1)}, u32[]{:S(2)}, u32[]{:S(2)}) collective-permute-start(bf16[272,128]{1,0:T(8,128)(2,1)S(1)} %get-tuple-element.137.refs_4_), channel_id=1, source_target_pairs={{0,96},{32,64},{64,32},{96,0},{1,97},{33,65},{65,33},{97,1},{2,98}... | collective-permute-start | bytes 208904 | tf_op jit(solution)/shard_map/ppermute | solution.py:649
  83.2 5.9 %collective-permute-start.23 = (bf16[256,128]{1,0:T(8,128)(2,1)S(1)}, bf16[256,128]{1,0:T(8,128)(2,1)S(1)}, u32[]{:S(2)}, u32[]{:S(2)}) collective-permute-start(bf16[256,128]{1,0:T(8,128)(2,1)S(1)} %get-tuple-element.141.refs_0_), channel_id=1, source_target_pairs={{0,64},{32,96},{64,0},{96,32},{1,65},{33,97},{65,1},{97,33},{2,66}... | collective-permute-start | bytes 196616 | tf_op jit(solution)/shard_map/ppermute | solution.py:649
  84.8 5.8 %collective-permute-start.24 = (bf16[256,128]{1,0:T(8,128)(2,1)S(1)}, bf16[256,128]{1,0:T(8,128)(2,1)S(1)}, u32[]{:S(2)}, u32[]{:S(2)}) collective-permute-start(bf16[256,128]{1,0:T(8,128)(2,1)S(1)} %get-tuple-element.141.refs_0_), channel_id=1, source_target_pairs={{0,96},{32,64},{64,32},{96,0},{1,97},{33,65},{65,33},{97,1},{2,98}... | collective-permute-start | bytes 196616 | tf_op jit(solution)/shard_map/ppermute | solution.py:649
  93.8 6.1 %collective-permute-start.25 = (bf16[256,128]{1,0:T(8,128)(2,1)S(1)}, bf16[256,128]{1,0:T(8,128)(2,1)S(1)}, u32[]{:S(2)}, u32[]{:S(2)}) collective-permute-start(bf16[256,128]{1,0:T(8,128)(2,1)S(1)} %get-tuple-element.158.refs_0_), channel_id=1, source_target_pairs={{0,32},{32,0},{64,96},{96,64},{1,33},{33,1},{65,97},{97,65},{2,34}... | collective-permute-start | bytes 196616 | tf_op jit(solution)/shard_map/ppermute | solution.py:649
  94.0 5.9 %collective-permute-start.26 = (bf16[256,128]{1,0:T(8,128)(2,1)S(1)}, bf16[256,128]{1,0:T(8,128)(2,1)S(1)}, u32[]{:S(2)}, u32[]{:S(2)}) collective-permute-start(bf16[256,128]{1,0:T(8,128)(2,1)S(1)} %get-tuple-element.158.refs_0_), channel_id=1, source_target_pairs={{0,64},{32,96},{64,0},{96,32},{1,65},{33,97},{65,1},{97,33},{2,66}... | collective-permute-start | bytes 196616 | tf_op jit(solution)/shard_map/ppermute | solution.py:649
  104.9 5.9 %collective-permute-start.29 = (bf16[256,128]{1,0:T(8,128)(2,1)S(1)}, bf16[256,128]{1,0:T(8,128)(2,1)S(1)}, u32[]{:S(2)}, u32[]{:S(2)}) collective-permute-start(bf16[256,128]{1,0:T(8,128)(2,1)S(1)} %get-tuple-element.169.refs_0_), channel_id=1, source_target_pairs={{0,64},{32,96},{64,0},{96,32},{1,65},{33,97},{65,1},{97,33},{2,66}... | collective-permute-start | bytes 196616 | tf_op jit(solution)/shard_map/ppermute | solution.py:649
  113.4 8.2 %collective-permute-start.38 = (bf16[2,32,1536]{2,1,0:T(8,128)(2,1)S(1)}, bf16[2,32,1536]{2,1,0:T(8,128)(2,1)S(1)}, u32[]{:S(2)}, u32[]{:S(2)}) collective-permute-start(bf16[2,32,1536]{2,1,0:T(8,128)(2,1)S(1)} %get-tuple-element.194), channel_id=1, source_target_pairs={{0,1},{1,2},{2,3},{3,0},{4,5},{5,6},{6,7},{7,4},{8,9},{9,10},{10,1... | collective-permute-start | bytes 589832 | tf_op jit(solution)/shard_map/ppermute | solution.py:587
  114.2 7.4 %collective-permute-start.39 = (bf16[2,32,1536]{2,1,0:T(8,128)(2,1)S(1)}, bf16[2,32,1536]{2,1,0:T(8,128)(2,1)S(1)}, u32[]{:S(2)}, u32[]{:S(2)}) collective-permute-start(bf16[2,32,1536]{2,1,0:T(8,128)(2,1)S(1)} %get-tuple-element.195), channel_id=1, source_target_pairs={{0,3},{1,0},{2,1},{3,2},{4,7},{5,4},{6,5},{7,6},{8,11},{9,8},{10,9... | collective-permute-start | bytes 589832 | tf_op jit(solution)/shard_map/ppermute | solution.py:587
  116.7 8.3 %collective-permute-start.31 = (bf16[2,384,128]{2,1,0:T(8,128)(2,1)S(1)}, bf16[2,384,128]{2,1,0:T(8,128)(2,1)S(1)}, u32[]{:S(2)}, u32[]{:S(2)}) collective-permute-start(bf16[2,384,128]{2,1,0:T(8,128)(2,1)S(1)} %get-tuple-element.183), channel_id=1, source_target_pairs={{0,8},{1,9},{2,10},{3,11},{4,12},{5,13},{6,14},{7,15},{8,16},{9,17... | collective-permute-start | bytes 589832 | tf_op jit(solution)/shard_map/ppermute | solution.py:583
  118.2 6.9 %collective-permute-start.32 = (bf16[2,384,128]{2,1,0:T(8,128)(2,1)S(1)}, bf16[2,384,128]{2,1,0:T(8,128)(2,1)S(1)}, u32[]{:S(2)}, u32[]{:S(2)}) collective-permute-start(bf16[2,384,128]{2,1,0:T(8,128)(2,1)S(1)} %get-tuple-element.184), channel_id=1, source_target_pairs={{0,24},{1,25},{2,26},{3,27},{4,28},{5,29},{6,30},{7,31},{8,0},{9,1... | collective-permute-start | bytes 589832 | tf_op jit(solution)/shard_map/ppermute | solution.py:583
  121.7 11.6 %collective-permute-start.40 = (bf16[4,32,1536]{2,1,0:T(8,128)(2,1)S(1)}, bf16[4,32,1536]{2,1,0:T(8,128)(2,1)S(1)}, u32[]{:S(2)}, u32[]{:S(2)}) collective-permute-start(bf16[4,32,1536]{2,1,0:T(8,128)(2,1)S(1)} %get-tuple-element.196), channel_id=1, source_target_pairs={{0,1},{1,2},{2,3},{3,0},{4,5},{5,6},{6,7},{7,4},{8,9},{9,10},{10,1... | collective-permute-start | bytes 1179656 | tf_op jit(solution)/shard_map/ppermute | solution.py:587
  123.2 10.1 %collective-permute-start.41 = (bf16[4,32,1536]{2,1,0:T(8,128)(2,1)S(1)}, bf16[4,32,1536]{2,1,0:T(8,128)(2,1)S(1)}, u32[]{:S(2)}, u32[]{:S(2)}) collective-permute-start(bf16[4,32,1536]{2,1,0:T(8,128)(2,1)S(1)} %get-tuple-element.197), channel_id=1, source_target_pairs={{0,3},{1,0},{2,1},{3,2},{4,7},{5,4},{6,5},{7,6},{8,11},{9,8},{10,9... | collective-permute-start | bytes 1179656 | tf_op jit(solution)/shard_map/ppermute | solution.py:587
  125.2 14.6 %collective-permute-start.33 = (bf16[4,384,128]{2,1,0:T(8,128)(2,1)S(1)}, bf16[4,384,128]{2,1,0:T(8,128)(2,1)S(1)}, u32[]{:S(2)}, u32[]{:S(2)}) collective-permute-start(bf16[4,384,128]{2,1,0:T(8,128)(2,1)S(1)} %get-tuple-element.185), channel_id=1, source_target_pairs={{0,8},{1,9},{2,10},{3,11},{4,12},{5,13},{6,14},{7,15},{8,16},{9,17... | collective-permute-start | bytes 1179656 | tf_op jit(solution)/shard_map/ppermute | solution.py:583
  126.7 13.1 %collective-permute-start.34 = (bf16[4,384,128]{2,1,0:T(8,128)(2,1)S(1)}, bf16[4,384,128]{2,1,0:T(8,128)(2,1)S(1)}, u32[]{:S(2)}, u32[]{:S(2)}) collective-permute-start(bf16[4,384,128]{2,1,0:T(8,128)(2,1)S(1)} %get-tuple-element.186), channel_id=1, source_target_pairs={{0,24},{1,25},{2,26},{3,27},{4,28},{5,29},{6,30},{7,31},{8,0},{9,1... | collective-permute-start | bytes 1179656 | tf_op jit(solution)/shard_map/ppermute | solution.py:583
  134.1 11.0 %collective-permute-start.42 = (bf16[4,32,384]{2,1,0:T(8,128)(2,1)S(1)}, bf16[4,32,384]{2,1,0:T(8,128)(2,1)S(1)}, u32[]{:S(2)}, u32[]{:S(2)}) collective-permute-start(bf16[4,32,384]{2,1,0:T(8,128)(2,1)S(1)} %get-tuple-element.199), channel_id=1, source_target_pairs={{0,8},{1,9},{2,10},{3,11},{4,12},{5,13},{6,14},{7,15},{8,16},{9,17... | collective-permute-start | bytes 294920 | tf_op jit(solution)/shard_map/ppermute | solution.py:583
  135.7 10.2 %collective-permute-start.43 = (bf16[4,32,384]{2,1,0:T(8,128)(2,1)S(1)}, bf16[4,32,384]{2,1,0:T(8,128)(2,1)S(1)}, u32[]{:S(2)}, u32[]{:S(2)}) collective-permute-start(bf16[4,32,384]{2,1,0:T(8,128)(2,1)S(1)} %get-tuple-element.200), channel_id=1, source_target_pairs={{0,16},{1,17},{2,18},{3,19},{4,20},{5,21},{6,22},{7,23},{8,24},{9,... | collective-permute-start | bytes 294920 | tf_op jit(solution)/shard_map/ppermute | solution.py:583
  138.4 7.6 %collective-permute-start.44 = (bf16[4,32,384]{2,1,0:T(8,128)(2,1)S(1)}, bf16[4,32,384]{2,1,0:T(8,128)(2,1)S(1)}, u32[]{:S(2)}, u32[]{:S(2)}) collective-permute-start(bf16[4,32,384]{2,1,0:T(8,128)(2,1)S(1)} %get-tuple-element.201), channel_id=1, source_target_pairs={{0,24},{1,25},{2,26},{3,27},{4,28},{5,29},{6,30},{7,31},{8,0},{9,1... | collective-permute-start | bytes 294920 | tf_op jit(solution)/shard_map/ppermute | solution.py:583
  140.6 5.9 %collective-permute-start.35 = (bf16[4,96,128]{2,1,0:T(8,128)(2,1)S(1)}, bf16[4,96,128]{2,1,0:T(8,128)(2,1)S(1)}, u32[]{:S(2)}, u32[]{:S(2)}) collective-permute-start(bf16[4,96,128]{2,1,0:T(8,128)(2,1)S(1)} %get-tuple-element.188), channel_id=1, source_target_pairs={{0,1},{1,2},{2,3},{3,0},{4,5},{5,6},{6,7},{7,4},{8,9},{9,10},{10,1... | collective-permute-start | bytes 294920 | tf_op jit(solution)/shard_map/ppermute | solution.py:587
  141.5 7.2 %collective-permute-start.36 = (bf16[4,96,128]{2,1,0:T(8,128)(2,1)S(1)}, bf16[4,96,128]{2,1,0:T(8,128)(2,1)S(1)}, u32[]{:S(2)}, u32[]{:S(2)}) collective-permute-start(bf16[4,96,128]{2,1,0:T(8,128)(2,1)S(1)} %get-tuple-element.189), channel_id=1, source_target_pairs={{0,2},{1,3},{2,0},{3,1},{4,6},{5,7},{6,4},{7,5},{8,10},{9,11},{10,... | collective-permute-start | bytes 294920 | tf_op jit(solution)/shard_map/ppermute | solution.py:587
  149.8 5.8 %collective-permute-start.45 = (bf16[4,192,128]{2,1,0:T(8,128)(2,1)S(1)}, bf16[4,192,128]{2,1,0:T(8,128)(2,1)S(1)}, u32[]{:S(2)}, u32[]{:S(2)}) collective-permute-start(bf16[4,192,128]{2,1,0:T(8,128)(2,1)S(1)} %shard_map.111), channel_id=1, source_target_pairs={{0,4},{1,5},{2,6},{3,7},{4,0},{5,1},{6,2},{7,3},{8,12},{9,13},{10,... | collective-permute-start | bytes 589832 | tf_op jit(solution)/shard_map/ppermute | solution.py:591
  155.8 5.7 %collective-permute-start.47 = (bf16[192,128]{1,0:T(8,128)(2,1)S(1)}, bf16[192,128]{1,0:T(8,128)(2,1)S(1)}, u32[]{:S(2)}, u32[]{:S(2)}) collective-permute-start(bf16[192,128]{1,0:T(8,128)(2,1)S(1)} %get-tuple-element.212), channel_id=1, source_target_pairs={{0,64},{32,96},{64,0},{96,32},{1,65},{33,97},{65,1},{97,33},{2,66}... | collective-permute-start | bytes 147464 | tf_op jit(solution)/shard_map/ppermute | solution.py:649
  163.0 8.2 %collective-permute-start.56 = (bf16[4,96,128]{2,1,0:T(8,128)(2,1)S(1)}, bf16[4,96,128]{2,1,0:T(8,128)(2,1)S(1)}, u32[]{:S(2)}, u32[]{:S(2)}) collective-permute-start(bf16[4,96,128]{2,1,0:T(8,128)(2,1)S(1)} %get-tuple-element.208), channel_id=1, source_target_pairs={{0,8},{1,9},{2,10},{3,11},{4,12},{5,13},{6,14},{7,15},{8,16},{9,17... | collective-permute-start | bytes 294920 | tf_op jit(solution)/shard_map/ppermute | solution.py:583
  163.7 8.3 %collective-permute-start.57 = (bf16[4,96,128]{2,1,0:T(8,128)(2,1)S(1)}, bf16[4,96,128]{2,1,0:T(8,128)(2,1)S(1)}, u32[]{:S(2)}, u32[]{:S(2)}) collective-permute-start(bf16[4,96,128]{2,1,0:T(8,128)(2,1)S(1)} %get-tuple-element.208), channel_id=1, source_target_pairs={{0,16},{1,17},{2,18},{3,19},{4,20},{5,21},{6,22},{7,23},{8,24},{9,... | collective-permute-start | bytes 294920 | tf_op jit(solution)/shard_map/ppermute | solution.py:583
  164.5 7.4 %collective-permute-start.58 = (bf16[4,96,128]{2,1,0:T(8,128)(2,1)S(1)}, bf16[4,96,128]{2,1,0:T(8,128)(2,1)S(1)}, u32[]{:S(2)}, u32[]{:S(2)}) collective-permute-start(bf16[4,96,128]{2,1,0:T(8,128)(2,1)S(1)} %get-tuple-element.208), channel_id=1, source_target_pairs={{0,24},{1,25},{2,26},{3,27},{4,28},{5,29},{6,30},{7,31},{8,0},{9,1... | collective-permute-start | bytes 294920 | tf_op jit(solution)/shard_map/ppermute | solution.py:583
  166.4 8.9 %collective-permute-start.50 = (bf16[4,96,128]{2,1,0:T(8,128)(2,1)S(1)}, bf16[4,96,128]{2,1,0:T(8,128)(2,1)S(1)}, u32[]{:S(2)}, u32[]{:S(2)}) collective-permute-start(bf16[4,96,128]{2,1,0:T(8,128)(2,1)S(1)} %get-tuple-element.209), channel_id=1, source_target_pairs={{0,2},{1,3},{2,0},{3,1},{4,6},{5,7},{6,4},{7,5},{8,10},{9,11},{10,... | collective-permute-start | bytes 294920 | tf_op jit(solution)/shard_map/ppermute | solution.py:587
  167.9 7.4 %collective-permute-start.51 = (bf16[4,96,128]{2,1,0:T(8,128)(2,1)S(1)}, bf16[4,96,128]{2,1,0:T(8,128)(2,1)S(1)}, u32[]{:S(2)}, u32[]{:S(2)}) collective-permute-start(bf16[4,96,128]{2,1,0:T(8,128)(2,1)S(1)} %get-tuple-element.209), channel_id=1, source_target_pairs={{0,3},{1,0},{2,1},{3,2},{4,7},{5,4},{6,5},{7,6},{8,11},{9,8},{10,9... | collective-permute-start | bytes 294920 | tf_op jit(solution)/shard_map/ppermute | solution.py:587
  171.2 6.9 %collective-permute-start.49 = (bf16[4,96,128]{2,1,0:T(8,128)(2,1)S(1)}, bf16[4,96,128]{2,1,0:T(8,128)(2,1)S(1)}, u32[]{:S(2)}, u32[]{:S(2)}) collective-permute-start(bf16[4,96,128]{2,1,0:T(8,128)(2,1)S(1)} %get-tuple-element.209), channel_id=1, source_target_pairs={{0,1},{1,2},{2,3},{3,0},{4,5},{5,6},{6,7},{7,4},{8,9},{9,10},{10,1... | collective-permute-start | bytes 294920 | tf_op jit(solution)/shard_map/ppermute | solution.py:587
  172.0 13.0 %collective-permute-start.59 = (bf16[4,4,96,128]{3,2,1,0:T(8,128)(2,1)S(1)}, bf16[4,4,96,128]{3,2,1,0:T(8,128)(2,1)S(1)}, u32[]{:S(2)}, u32[]{:S(2)}) collective-permute-start(bf16[4,4,96,128]{3,2,1,0:T(8,128)(2,1)S(1)} %pad_maximum_fusion.3.refs_3_), channel_id=1, source_target_pairs={{0,1},{1,2},{2,3},{3,0},{4,5},{5,6},{6,7},{7,4},{8,9},{9,10},{10,1... | collective-permute-start | bytes 1179656 | tf_op jit(solution)/shard_map/ppermute | solution.py:587
  172.8 12.3 %collective-permute-start.61 = (bf16[4,4,96,128]{3,2,1,0:T(8,128)(2,1)S(1)}, bf16[4,4,96,128]{3,2,1,0:T(8,128)(2,1)S(1)}, u32[]{:S(2)}, u32[]{:S(2)}) collective-permute-start(bf16[4,4,96,128]{3,2,1,0:T(8,128)(2,1)S(1)} %pad_maximum_fusion.3.refs_3_), channel_id=1, source_target_pairs={{0,3},{1,0},{2,1},{3,2},{4,7},{5,4},{6,5},{7,6},{8,11},{9,8},{10,9... | collective-permute-start | bytes 1179656 | tf_op jit(solution)/shard_map/ppermute | solution.py:587
  178.2 10.2 %collective-permute-start.52 = (bf16[4,4,96,128]{3,2,1,0:T(8,128)(2,1)S(1)}, bf16[4,4,96,128]{3,2,1,0:T(8,128)(2,1)S(1)}, u32[]{:S(2)}, u32[]{:S(2)}) collective-permute-start(bf16[4,4,96,128]{3,2,1,0:T(8,128)(2,1)S(1)} %pad_maximum_fusion.2.refs_0_), channel_id=1, source_target_pairs={{0,8},{1,9},{2,10},{3,11},{4,12},{5,13},{6,14},{7,15},{8,16},{9,17... | collective-permute-start | bytes 1179656 | tf_op jit(solution)/shard_map/ppermute | solution.py:583
  178.3 10.2 %collective-permute-start.54 = (bf16[4,4,96,128]{3,2,1,0:T(8,128)(2,1)S(1)}, bf16[4,4,96,128]{3,2,1,0:T(8,128)(2,1)S(1)}, u32[]{:S(2)}, u32[]{:S(2)}) collective-permute-start(bf16[4,4,96,128]{3,2,1,0:T(8,128)(2,1)S(1)} %pad_maximum_fusion.2.refs_0_), channel_id=1, source_target_pairs={{0,24},{1,25},{2,26},{3,27},{4,28},{5,29},{6,30},{7,31},{8,0},{9,1... | collective-permute-start | bytes 1179656 | tf_op jit(solution)/shard_map/ppermute | solution.py:583
  185.0 9.2 %collective-permute-start.60 = (bf16[2,4,96,128]{3,2,1,0:T(8,128)(2,1)S(1)}, bf16[2,4,96,128]{3,2,1,0:T(8,128)(2,1)S(1)}, u32[]{:S(2)}, u32[]{:S(2)}) collective-permute-start(bf16[2,4,96,128]{3,2,1,0:T(8,128)(2,1)S(1)} %slice.36), channel_id=1, source_target_pairs={{0,1},{1,2},{2,3},{3,0},{4,5},{5,6},{6,7},{7,4},{8,9},{9,10},{10,1... | collective-permute-start | bytes 589832 | tf_op jit(solution)/shard_map/ppermute | solution.py:587
  185.1 9.1 %collective-permute-start.62 = (bf16[2,4,96,128]{3,2,1,0:T(8,128)(2,1)S(1)}, bf16[2,4,96,128]{3,2,1,0:T(8,128)(2,1)S(1)}, u32[]{:S(2)}, u32[]{:S(2)}) collective-permute-start(bf16[2,4,96,128]{3,2,1,0:T(8,128)(2,1)S(1)} %slice.37), channel_id=1, source_target_pairs={{0,3},{1,0},{2,1},{3,2},{4,7},{5,4},{6,5},{7,6},{8,11},{9,8},{10,9... | collective-permute-start | bytes 589832 | tf_op jit(solution)/shard_map/ppermute | solution.py:587
  188.4 7.0 %collective-permute-start.53 = (bf16[2,4,96,128]{3,2,1,0:T(8,128)(2,1)S(1)}, bf16[2,4,96,128]{3,2,1,0:T(8,128)(2,1)S(1)}, u32[]{:S(2)}, u32[]{:S(2)}) collective-permute-start(bf16[2,4,96,128]{3,2,1,0:T(8,128)(2,1)S(1)} %slice.33), channel_id=1, source_target_pairs={{0,8},{1,9},{2,10},{3,11},{4,12},{5,13},{6,14},{7,15},{8,16},{9,17... | collective-permute-start | bytes 589832 | tf_op jit(solution)/shard_map/ppermute | solution.py:583
  188.5 6.8 %collective-permute-start.55 = (bf16[2,4,96,128]{3,2,1,0:T(8,128)(2,1)S(1)}, bf16[2,4,96,128]{3,2,1,0:T(8,128)(2,1)S(1)}, u32[]{:S(2)}, u32[]{:S(2)}) collective-permute-start(bf16[2,4,96,128]{3,2,1,0:T(8,128)(2,1)S(1)} %slice.34), channel_id=1, source_target_pairs={{0,24},{1,25},{2,26},{3,27},{4,28},{5,29},{6,30},{7,31},{8,0},{9,1... | collective-permute-start | bytes 589832 | tf_op jit(solution)/shard_map/ppermute | solution.py:583
  (15 other events, 60.2 us)
